TPU v7x, 32 devices: a whole 2x2x4 slice. The times are simulated.
32 devices in a mesh: row: 8 (over z, core), col: 4 (over y, x).
Axes of the slice: x: 2, y: 2, z: 4, core: 2. Of those that a mesh axis runs over, the one named last changes fastest.
Arguments:
- train_points: float32 [64, 2048], P(None, ('row', 'col')), may hold values from -6 to 6
- cand_points: float32 [64, 2048], P(None, ('row', 'col')), may hold values from -6 to 6
- inv_length: float32 [64], replicated, may hold values from 0.04 to 0.7
- noise: float32 [2048], P(('row', 'col')), may hold values from 0.5 to 4
- targets: float32 [16, 2048], P(None, ('row', 'col')), may hold values from -15 to 15
Outputs:
- solution: float32 [16, 2048], P(None, ('row', 'col'))
- post_mean: float32 [16, 2048], P(None, ('row', 'col'))
All inputs are finite; a program needn't handle non-finite values.
Results may differ from a plain program's by a relative error of at most 0.0047.
Values may be sent and summed in bfloat16 or wider, within the bound.
A program may use at most 64 MiB of HBM per device.

v0:
```python
import math

import jax
import jax.numpy as jnp
from jax import lax
from jax.sharding import PartitionSpec as P

ITERS = 2


root_five = math.sqrt(5.0)


def matern(left, left_norm, right, right_norm):
    inner = lax.dot_general(
        left, right, (((0,), (0,)), ((), ())), preferred_element_type=jnp.float32
    )
    dist_sq = jnp.maximum(left_norm[:, None] + right_norm[None, :] - 2.0 * inner, 0.0)
    radius = jnp.sqrt(dist_sq)
    return (1.0 + root_five * radius + 5.0 / 3.0 * dist_sq) * jnp.exp(-root_five * radius)


def tile_rows(amount):
    if amount <= 512:
        return amount
    best = 1
    for candidate in range(1, 513):
        if amount % candidate == 0:
            best = candidate
    return best


def accumulate(carried, vector_piece, piece_points, piece_norms, other, other_norms):
    amount = vector_piece.shape[1]
    block = tile_rows(amount)

    def advance(block_index, running):
        offset = block_index * block
        sub_points = lax.dynamic_slice_in_dim(piece_points, offset, block, 1)
        sub_norms = lax.dynamic_slice_in_dim(piece_norms, offset, block, 0)
        sub_vector = lax.dynamic_slice_in_dim(vector_piece, offset, block, 1)
        kernel_tile = matern(sub_points, sub_norms, other, other_norms)
        return running + jnp.dot(
            sub_vector,
            kernel_tile,
            precision=lax.Precision.HIGHEST,
            preferred_element_type=jnp.float32,
        )

    return lax.fori_loop(0, amount // block, advance, carried)


def per_device(train_points, cand_points, inv_length, noise, targets):
    scaled_train = (train_points * inv_length[:, None]).astype(jnp.bfloat16)
    scaled_cand = (cand_points * inv_length[:, None]).astype(jnp.bfloat16)
    row_train, row_cand = (
        lax.all_gather(scaled_train, "col", axis=1, tiled=True),
        lax.all_gather(scaled_cand, "col", axis=1, tiled=True),
    )
    col_train = lax.all_gather(scaled_train, "row", axis=1, tiled=True)
    row_norms = jnp.sum(jnp.square(row_train.astype(jnp.float32)), axis=0)
    cand_norms = jnp.sum(jnp.square(row_cand.astype(jnp.float32)), axis=0)
    col_norms = jnp.sum(jnp.square(col_train.astype(jnp.float32)), axis=0)
    outputs = targets.shape[0]

    def from_columns(other, other_norms, carried, vector_piece):
        return accumulate(carried, vector_piece, col_train, col_norms, other, other_norms)

    def squares(residual):
        return lax.psum(jnp.sum(residual * residual, axis=1), ("row", "col"))

    solution = jnp.zeros_like(targets)
    residual = targets
    direction = targets
    norm_now = squares(residual)
    for iteration in range(ITERS):
        start_total = jnp.zeros((outputs, row_train.shape[1]), jnp.float32)
        partial_image = from_columns(
            row_train, row_norms, start_total, lax.all_gather(direction, "row", axis=1, tiled=True)
        )
        own_image = lax.psum_scatter(partial_image, "col", scatter_dimension=1, tiled=True)
        image = own_image + noise[None, :] * direction
        alpha = norm_now / lax.psum(jnp.sum(direction * image, axis=1), ("row", "col"))
        solution = solution + alpha[:, None] * direction
        residual = residual - alpha[:, None] * image
        norm_next = squares(residual)
        direction = residual + (norm_next / norm_now)[:, None] * direction
        norm_now = norm_next
    mean_start = jnp.zeros((outputs, row_cand.shape[1]), jnp.float32)
    partial_mean = from_columns(
        row_cand, cand_norms, mean_start, lax.all_gather(solution, "row", axis=1, tiled=True)
    )
    post_mean = lax.psum_scatter(partial_mean, "col", scatter_dimension=1, tiled=True)
    return (solution, post_mean)


def solution(mesh):
    placed = (
        P(None, ("row", "col")),
        P(None, ("row", "col")),
        P(),
        P(("row", "col")),
        P(None, ("row", "col")),
    )
    return jax.shard_map(
        per_device,
        mesh=mesh,
        in_specs=placed,
        out_specs=(P(None, ("row", "col")), P(None, ("row", "col"))),
        check_vma=False,
    )
```

profile of v0, /device:TPU:0, one launch (start us, length us, event | category | flops | bytes accessed | tf_op | source)
XLA Modules:
  0.0 291.7 jit_solution(17940625280633191751)
XLA Ops:
  7.2 0.8 copy.10
  8.1 0.6 copy-done.4
  8.7 15.7 %all_gather.18 = bf16[64,512]{0,1:T(8,128)(2,1)S(1)} all-gather(bf16[64,64]{0,1:T(8,128)(2,1)S(1)} %get-tuple-element.55), channel_id=1, replica_groups=mesh['row'=8,'col'=4] {'row'}, dimensions={1}, use_global_device_ids=true | all-gather | bytes 73728 | tf_op jit(solution)/shard_map/all_gather | solution.py:60
  24.4 8.2 %all_gather.19 = bf16[64,256]{0,1:T(8,128)(2,1)S(1)} all-gather(bf16[64,64]{0,1:T(8,128)(2,1)S(1)} %get-tuple-element.55), channel_id=1, replica_groups=mesh['row'=8,'col'=4] {'col'}, dimensions={1}, use_global_device_ids=true | all-gather | bytes 40960 | tf_op jit(solution)/shard_map/all_gather | solution.py:57
  33.0 0.6 copy-done
  33.5 14.0 %all-gather = f32[8,64,16]{1,2,0:T(8,128)S(1)} all-gather(f32[1,64,16]{1,2,0:T(8,128)S(1)} %bitcast.36), channel_id=1, replica_groups=mesh['row'=8,'col'=4] {'row'}, dimensions={0}, use_global_device_ids=true | all-gather | bytes 36864 | tf_op jit(solution)/shard_map/all_gather | solution.py:79
  47.6 0.5 exponential_multiply_fusion
  48.1 0.4 convolution_bitcast_fusion.2
  48.5 0.7 copy.15
  49.3 24.0 %reduce-scatter.10.cloned.1.call-done = f32[64,16]{1,0:T(8,128)} async-done(((f32[256,16]{1,0:T(8,128)}), f32[64,16]{1,0:T(8,128)}) %reduce-scatter.10.cloned.1.call-update) | async-done | bytes 4112
  73.2 0.8 copy.16
  74.2 39.4 %all-reduce = (f32[16]{0:T(128)S(1)}, f32[16]{0:T(128)S(1)}) all-reduce(f32[16]{0:T(128)S(1)} %get-tuple-element.51, f32[16]{0:T(128)S(1)} %get-tuple-element.50), channel_id=1, replica_groups=mesh['row'=8,'col'=4] {'row','col'}, use_global_device_ids=true, to_apply=%region_1.0 | all-reduce | flops 32 | bytes 256 | tf_op jit(solution)/shard_map/psum | solution.py:70
  113.7 9.0 %all_gather.23 = bf16[64,256]{0,1:T(8,128)(2,1)S(1)} all-gather(bf16[64,64]{0,1:T(8,128)(2,1)S(1)} %get-tuple-element.54), channel_id=1, replica_groups=mesh['row'=8,'col'=4] {'col'}, dimensions={1}, use_global_device_ids=true | all-gather | bytes 40960 | tf_op jit(solution)/shard_map/all_gather | solution.py:58
  122.7 39.2 %psum.30 = f32[16]{0:T(128)S(1)} all-reduce(f32[16]{0:T(128)S(1)} %multiply_reduce_fusion.4), channel_id=1, replica_groups=mesh['row'=8,'col'=4] {'row','col'}, use_global_device_ids=true, to_apply=%region_8.0 | all-reduce | flops 16 | bytes 128 | tf_op jit(solution)/shard_map/psum | solution.py:70
  162.0 14.0 %all-gather.1 = f32[8,64,16]{1,2,0:T(8,128)S(1)} all-gather(f32[1,64,16]{1,2,0:T(8,128)S(1)} %fusion.20), channel_id=1, replica_groups=mesh['row'=8,'col'=4] {'row'}, dimensions={0}, use_global_device_ids=true | all-gather | bytes 36864 | tf_op jit(solution)/shard_map/all_gather | solution.py:79
  176.1 1.6 convolution_bitcast_fusion.1
  177.9 24.6 %reduce-scatter.12.cloned.1.call-done = f32[64,16]{1,0:T(8,128)} async-done(((f32[256,16]{1,0:T(8,128)}), f32[64,16]{1,0:T(8,128)}) %reduce-scatter.12.cloned.1.call-update) | async-done | bytes 4112
  202.5 0.8 copy.18
  203.5 0.2 fusion.3
  203.8 39.4 %psum.31 = f32[16]{0:T(128)S(1)} all-reduce(f32[16]{0:T(128)S(1)} %multiply_reduce_fusion.3), channel_id=1, replica_groups=mesh['row'=8,'col'=4] {'row','col'}, use_global_device_ids=true, to_apply=%region_11.0 | all-reduce | flops 16 | bytes 128 | tf_op jit(solution)/shard_map/psum | solution.py:83
  243.2 14.0 %all-gather.2 = f32[8,64,16]{1,2,0:T(8,128)S(1)} all-gather(f32[1,64,16]{1,2,0:T(8,128)S(1)} %bitcast.40), channel_id=1, replica_groups=mesh['row'=8,'col'=4] {'row'}, dimensions={0}, use_global_device_ids=true | all-gather | bytes 36864 | tf_op jit(solution)/shard_map/all_gather | solution.py:91
  257.3 1.8 convolution_bitcast_fusion
  259.1 24.6 %reduce-scatter.14.cloned.1.call-done = f32[64,16]{1,0:T(8,128)} async-done(((f32[256,16]{1,0:T(8,128)}), f32[64,16]{1,0:T(8,128)}) %reduce-scatter.14.cloned.1.call-update) | async-done | bytes 4112
  283.7 1.4 copy.20
  (33 shorter events, 1.6 us)
Async XLA Ops:
  7.2 0.9 copy-start.2
  7.2 66.0 %reduce-scatter.10.cloned.1.call-start = ((), (), s32[]{:S(2)}) async-start(), calls=%async_computation.3 | async-start | bytes 163840
  8.1 0.7 copy-start.4
  32.8 0.7 copy-start
  49.2 153.3 %reduce-scatter.12.cloned.1.call-start = ((), (), s32[]{:S(2)}) async-start(), calls=%async_computation.4 | async-start | bytes 163840
  73.2 0.8 copy-start.3
  177.8 106.0 %reduce-scatter.14.cloned.1.call-start = ((), (), s32[]{:S(2)}) async-start(), calls=%async_computation.5 | async-start | bytes 163840
  243.2 14.0 %copy-start.1 = (f32[16,64]{1,0:T(8,128)}, f32[16,64]{1,0:T(8,128)S(1)}, u32[]{:S(2)}) copy-start(f32[16,64]{1,0:T(8,128)S(1)} %multiply_add_fusion) | copy-start | bytes 12292
Sparse Core Ops, SparseCore 0:
  49.3 23.8 reduce-scatter.9
  177.9 24.5 reduce-scatter.11
  259.2 24.4 reduce-scatter.13
where the time goes:
time: 292 us
  blocking collectives  193 us (66%)
  waiting for transfers between devices  73.2 us (25%)
  between operations  13.8 us (5%)
  local copies, waits for them, and re-layouts  6.18 us (2%)
  matrix products  4.49 us (2%)
    psum x2, blocking collectives, squares(): return lax.psum(jnp.sum(residual * residual, axis=1), ('row', 'col'))  78.6 us
    unnamed x6, waiting for transfers between devices  73.2 us
    psum x1, blocking collectives, per_device(): lax.psum(jnp.sum(direction * image, axis=1), ('row', 'col'))  39.4 us
    all_gather x2, blocking collectives, per_device(): lax.all_gather(direction, 'row', axis=1, tiled=True)  27.9 us
    all_gather x1, blocking collectives, per_device(): col_train = lax.all_gather(scaled_train, 'row', axis=1, tiled=True)  15.7 us
    all_gather x1, blocking collectives, per_device(): lax.all_gather(solution, 'row', axis=1, tiled=True)  14 us
    all_gather x1, blocking collectives, per_device(): lax.all_gather(scaled_cand, 'col', axis=1, tiled=True)  9 us
    all_gather x1, blocking collectives, per_device(): lax.all_gather(scaled_train, 'col', axis=1, tiled=True)  8.23 us
  transfers between devices with their start and end apart: 3, of which 3 were waited for; matrix products, arithmetic and copies ran while one was open for 0% of the time, Pallas kernels for 0%

commit v1 on v0

v1 whole, which is shorter than its diff:
```python
import functools
import math

import jax
import jax.numpy as jnp
from jax import lax
from jax.experimental import pallas as pl
from jax.experimental.pallas import tpu as pltpu
from jax.sharding import PartitionSpec as P

MESH = pl.DeviceIdType.MESH
root_five = math.sqrt(5.0)
F32 = jnp.float32
BF16 = jnp.bfloat16


def lanes_of(rows):
    return lax.broadcasted_iota(jnp.int32, (rows, 128), 1)


def rounded(value):
    return value.astype(BF16).astype(F32)


def halves(doubled):
    high = rounded(doubled)
    return jnp.where(lanes_of(doubled.shape[0]) < 64, high, doubled - high).astype(BF16)


def whole(block):
    value = block.astype(F32)
    return value + pltpu.roll(value, 64, 1)


def doubled(value):
    return jnp.where(lanes_of(value.shape[0]) < 64, value, pltpu.roll(value, 64, 1))


def point_forms(points):
    amount, dims = points.shape
    norm = jnp.sum(points * points, axis=1, keepdims=True)
    high = rounded(norm)
    middle = rounded(norm - high)
    low = rounded(norm - high - middle)
    lane = lanes_of(amount)
    padded = jnp.concatenate([points, jnp.zeros((amount, 128 - dims), F32)], axis=1)
    left, right = padded, -2.0 * padded
    for place, part in enumerate((high, middle, low)):
        left = jnp.where(lane == dims + place, part, left)
        left = jnp.where(lane == dims + 3 + place, 1.0, left)
        right = jnp.where(lane == dims + place, 1.0, right)
        right = jnp.where(lane == dims + 3 + place, part, right)
    return left.astype(BF16), right.astype(BF16)


def matern_split(left, right):
    dist = lax.dot_general(
        left, right, (((1,), (1,)), ((), ())), preferred_element_type=F32
    )
    dist = jnp.maximum(dist, 0.0)
    scaled = root_five * dist * lax.rsqrt(jnp.maximum(dist, 1e-30))
    kern = (1.0 + scaled + (5.0 / 3.0) * dist) * jnp.exp(-scaled)
    high = kern.astype(BF16)
    return high, (kern - high.astype(F32)).astype(BF16)


def apply_tile(block, high, low):
    return jnp.dot(
        jnp.concatenate([block, block], axis=1),
        jnp.concatenate([high, high, low, low], axis=0),
        preferred_element_type=F32,
    )


def column(value, lane_at):
    return jnp.sum(
        jnp.where(lanes_of(value.shape[0]) == lane_at, value, 0.0), axis=1, keepdims=True
    )


def kernel(
    rows, cols,
    train_ref, cand_ref, inv_ref, noise_ref, target_ref,
    solution_ref, mean_ref,
    ibuf, jbuf, cbuf, ktrain, kcand, psend, pbuf, vown, vrow, vcol, wsend, wbuf, sbuf,
    i_send, i_recv, j_send, j_recv, c_send, c_recv, p_send, p_recv,
    vr_send, vr_recv, vc_send, vc_recv, w_send, w_recv, s_send, s_recv,
):
    a = lax.axis_index("row")
    b = lax.axis_index("col")
    row_peers = [lax.rem(a + k, rows) for k in range(1, rows)]
    col_peers = [lax.rem(b + k, cols) for k in range(1, cols)]

    barrier = pltpu.get_barrier_semaphore()
    for p in row_peers:
        pl.semaphore_signal(barrier, inc=1, device_id=(p, b), device_id_type=MESH)
    for p in col_peers:
        pl.semaphore_signal(barrier, inc=1, device_id=(a, p), device_id_type=MESH)

    def to_row(src, buf, send, recv):
        return [
            pltpu.make_async_remote_copy(
                src_ref=src, dst_ref=buf.at[a], send_sem=send.at[p], recv_sem=recv.at[a],
                device_id=(p, b), device_id_type=MESH,
            )
            for p in row_peers
        ]

    def to_col(src, buf, send, recv):
        return [
            pltpu.make_async_remote_copy(
                src_ref=src(p), dst_ref=buf.at[b], send_sem=send.at[p], recv_sem=recv.at[b],
                device_id=(a, p), device_id_type=MESH,
            )
            for p in col_peers
        ]

    def arrived(buf, recv, p):
        pltpu.make_async_remote_copy(
            src_ref=buf.at[p], dst_ref=buf.at[p], send_sem=recv.at[p], recv_sem=recv.at[p],
            device_id=(a, b), device_id_type=MESH,
        ).wait_recv()

    lane = lanes_of(16)
    left_half = lane < 64

    points = jnp.concatenate([train_ref[...], cand_ref[...]], axis=1).T * inv_ref[...]
    left, right = point_forms(rounded(points))
    own_points = train_ref.shape[1]
    target = target_ref[...]
    target2 = jnp.concatenate([target, target], axis=1)
    target_block = halves(target2)
    noise = noise_ref[...]
    noise2 = jnp.concatenate([noise, noise], axis=1)
    ibuf[a, 0:64, :] = left[:own_points]
    ibuf[a, 64:80, :] = target_block
    jbuf[b, 0:64, :] = right[:own_points]
    jbuf[b, 64:80, :] = target_block
    cbuf[b] = right[own_points:]

    pl.semaphore_wait(barrier, rows + cols - 2)
    sent = to_row(ibuf.at[a], ibuf, i_send, i_recv)
    sent += to_col(lambda p: jbuf.at[b], jbuf, j_send, j_recv)
    sent += to_col(lambda p: cbuf.at[b], cbuf, c_send, c_recv)
    for copy in sent:
        copy.start()

    for p in col_peers:
        arrived(jbuf, j_recv, p)
    right_train = jbuf[:, 0:64, :].reshape(cols * 64, 128)
    partial = jnp.zeros((16, cols * 64), F32)
    for k in range(rows):
        p = a if k == 0 else row_peers[k - 1]
        if k:
            arrived(ibuf, i_recv, p)
        high, low = matern_split(ibuf[p, 0:64, :], right_train)
        ktrain[p, 0:64, :] = high
        ktrain[p, 64:128, :] = low
        partial += apply_tile(ibuf[p, 64:80, :], high, low)

    def over_columns(block_of):
        return [
            jnp.where(left_half, block_of(2 * h), block_of(2 * h + 1))
            for h in range(cols // 2)
        ]

    target_cols = over_columns(lambda s: whole(jbuf[s, 64:80, :]))

    def inner(wide, blocks):
        total = jnp.zeros((16, 128), F32)
        for h, block in enumerate(blocks):
            total += wide[:, 128 * h : 128 * h + 128] * block
        return jnp.sum(total, axis=1, keepdims=True)

    own_bb = jnp.sum(target * target, axis=1, keepdims=True)
    own_bnb = jnp.sum(noise * target * target, axis=1, keepdims=True)
    scalars = jnp.where(
        lane == 64, inner(partial, target_cols) + own_bnb, jnp.where(lane == 65, own_bb, 0.0)
    )
    for s in range(cols):
        piece = partial[:, 128 * (s // 2) : 128 * (s // 2) + 128]
        if s % 2:
            piece = pltpu.roll(piece, 64, 1)
        psend[s] = jnp.where(left_half, piece, scalars)
    copies = to_col(lambda p: psend.at[p], pbuf, p_send, p_recv)
    for copy in copies:
        copy.start()
    sent += copies

    for p in col_peers:
        arrived(cbuf, c_recv, p)
    right_cand = cbuf[...].reshape(cols * 64, 128)
    mean_b = jnp.zeros((16, cols * 64), F32)
    for k in range(rows):
        high, low = matern_split(ibuf[k, 0:64, :], right_cand)
        kcand[k, 0:64, :] = high
        kcand[k, 64:128, :] = low
        mean_b += apply_tile(ibuf[k, 64:80, :], high, low)

    image = psend[b]
    for p in col_peers:
        arrived(pbuf, p_recv, p)
        image += pbuf[p]
    value = image + jnp.where(left_half, noise2 * target2, 0.0)
    vrow[a] = value
    vcol[b] = value
    copies = to_row(vrow.at[a], vrow, vr_send, vr_recv)
    copies += to_col(lambda p: vcol.at[b], vcol, vc_send, vc_recv)
    for copy in copies:
        copy.start()
    sent += copies
    for p in row_peers:
        arrived(vrow, vr_recv, p)
    totals = vrow[0]
    for k in range(1, rows):
        totals += vrow[k]
    b_a_b = column(totals, 64)
    b_b = column(totals, 65)
    alpha = b_b / b_a_b

    image_r = jnp.zeros((16, cols * 64), F32)
    mean_r = jnp.zeros((16, cols * 64), F32)
    for k in range(rows):
        residual = whole(ibuf[k, 64:80, :]) - alpha * doubled(vrow[k])
        block = halves(residual)
        image_r += apply_tile(block, ktrain[k, 0:64, :], ktrain[k, 64:128, :])
        mean_r += apply_tile(block, kcand[k, 0:64, :], kcand[k, 64:128, :])
    for p in col_peers:
        arrived(vcol, vc_recv, p)
    residual_cols = over_columns(
        lambda s: whole(jbuf[s, 64:80, :]) - alpha * doubled(vcol[s])
    )
    value_own = value[:, 0:64]
    residual_own = target - alpha * value_own
    square = residual_own * residual_own
    own_rar = inner(image_r, residual_cols) + jnp.sum(noise * square, axis=1, keepdims=True)
    own_rr = jnp.sum(square, axis=1, keepdims=True)
    own_vr = jnp.sum(value_own * residual_own, axis=1, keepdims=True)
    scalars = jnp.where(
        lane == 0, own_rar, jnp.where(lane == 1, own_rr, jnp.where(lane == 2, own_vr, 0.0))
    )
    for s in range(cols):
        at = 128 * (s // 2)
        first, second = mean_b[:, at : at + 128], mean_r[:, at : at + 128]
        if s % 2:
            first = pltpu.roll(first, 64, 1)
        else:
            second = pltpu.roll(second, 64, 1)
        wsend[s, :, 0:128] = jnp.where(left_half, first, second)
        wsend[s, :, 128:256] = scalars
    copies = to_col(lambda p: wsend.at[p], wbuf, w_send, w_recv)
    for copy in copies:
        copy.start()
    sent += copies
    means = wsend[b]
    for p in col_peers:
        arrived(wbuf, w_recv, p)
        means += wbuf[p]
    scalars = means[:, 128:256]
    row_at = lax.broadcasted_iota(jnp.int32, (16, 128), 0)
    spread = jnp.zeros((16, 128), F32)
    for q in range(3):
        spread = jnp.where(lane == row_at + 16 * q, column(scalars, q), spread)
    packed = jnp.sum(spread, axis=0, keepdims=True)
    sbuf[a] = jnp.broadcast_to(packed, (8, 128))
    copies = to_row(sbuf.at[a], sbuf, s_send, s_recv)
    for copy in copies:
        copy.start()
    sent += copies
    for p in row_peers:
        arrived(sbuf, s_recv, p)
    totals = sbuf[0]
    for k in range(1, rows):
        totals += sbuf[k]
    totals = jnp.concatenate([totals, totals], axis=0)

    def unpacked(q):
        return jnp.sum(
            jnp.where(lane == row_at + 16 * q, totals, 0.0), axis=1, keepdims=True
        )

    r_a_r, fresh, v_r = unpacked(0), unpacked(1), unpacked(2)
    beta = fresh / b_b
    curve = r_a_r + 2.0 * beta * v_r + beta * beta * b_a_b
    alpha_two = fresh / curve
    share = alpha + alpha_two * beta
    solution_ref[...] = share * target + alpha_two * residual_own
    mean_ref[...] = share * means[:, 0:64] + alpha_two * means[:, 64:128]
    for copy in sent:
        copy.wait_send()


def per_device(rows, cols, train_points, cand_points, inv_length, noise, targets):
    vmem = pl.BlockSpec(memory_space=pltpu.VMEM)
    out = jax.ShapeDtypeStruct(targets.shape, F32)
    dma = pltpu.SemaphoreType.DMA
    width = cols * 64
    by_row, by_col = dma((rows,)), dma((cols,))
    return pl.pallas_call(
        functools.partial(kernel, rows, cols),
        out_shape=(out, out),
        in_specs=[vmem] * 5,
        out_specs=(vmem, vmem),
        scratch_shapes=[
            pltpu.VMEM((rows, 80, 128), BF16),
            pltpu.VMEM((cols, 80, 128), BF16),
            pltpu.VMEM((cols, 64, 128), BF16),
            pltpu.VMEM((rows, 128, width), BF16),
            pltpu.VMEM((rows, 128, width), BF16),
            pltpu.VMEM((cols, 16, 128), F32),
            pltpu.VMEM((cols, 16, 128), F32),
            pltpu.VMEM((1, 8, 128), F32),
            pltpu.VMEM((rows, 16, 128), F32),
            pltpu.VMEM((cols, 16, 128), F32),
            pltpu.VMEM((cols, 16, 256), F32),
            pltpu.VMEM((cols, 16, 256), F32),
            pltpu.VMEM((rows, 8, 128), F32),
            by_row, by_row, by_col, by_col, by_col, by_col, by_col, by_col,
            by_row, by_row, by_col, by_col, by_col, by_col, by_row, by_row,
        ],
        compiler_params=pltpu.CompilerParams(
            collective_id=0, has_side_effects=True, vmem_limit_bytes=40 * 1024 * 1024
        ),
    )(train_points, cand_points, inv_length.reshape(1, -1), noise.reshape(1, -1), targets)


def solution(mesh):
    placed = (
        P(None, ("row", "col")),
        P(None, ("row", "col")),
        P(),
        P(("row", "col")),
        P(None, ("row", "col")),
    )
    return jax.shard_map(
        functools.partial(per_device, mesh.shape["row"], mesh.shape["col"]),
        mesh=mesh,
        in_specs=placed,
        out_specs=(P(None, ("row", "col")), P(None, ("row", "col"))),
        check_vma=False,
    )
```

time: 292 us -> 32.1 us (0.11)
  blocking collectives: 193 us -> 0 us
  waiting for transfers between devices: 73.2 us -> 0 us
  Pallas kernels: 0 us -> 27 us
  between operations: 13.8 us -> 0.66 us
  matrix products: 4.49 us -> 0 us
    psum x3 -> x0, blocking collectives: 118 us -> none  [the longest x2 78.6 us: squares(): return lax.psum(jnp.sum(residual * residual, axis=1), ('row', 'col'))]
    all_gather x6 -> x0, blocking collectives: 74.8 us -> none  [the longest x2 27.9 us: per_device(): lax.all_gather(direction, 'row', axis=1, tiled=True)]
    unnamed x6 -> x0, waiting for transfers between devices: 73.2 us -> none
    pallas_call x0 -> x1, Pallas kernels: none -> 27 us  [per_device(): pl.pallas_call(functools.partial(kernel, rows, cols), out_shape=(out, out...]
    unnamed x2 -> x0, matrix products: 3.4 us -> none
    unnamed x19 -> x12, local copies, waits for them, and re-layouts: 6.11 us -> 4.07 us
  transfers between devices with their start and end apart: 3 -> 0, of which waited for: 3 -> 0; matrix products, arithmetic and copies ran while one was open for 0% -> 0% of each run, Pallas kernels for 0% -> 0%
where the time goes in v1:
time: 32.1 us; the launch traced here: 31.8 us
  Pallas kernels  27 us (84%)
  local copies, waits for them, and re-layouts  4.07 us (13%)
  between operations  0.66 us (2%)
    pallas_call x1, Pallas kernels, per_device(): pl.pallas_call(functools.partial(kernel, rows, cols), out_shape=(out, out...  27 us
    unnamed x12, local copies, waits for them, and re-layouts  4.07 us

profile of v1, /device:TPU:0, one launch (start us, length us, event | category | flops | bytes accessed | tf_op | source)
XLA Modules:
  0.0 31.8 jit_solution(2259870949287882758)
XLA Ops:
  0.6 0.0 copy-start.3
  0.6 0.0 copy-start.4
  0.7 0.6 %copy-done.3 = f32[64]{0:T(128)S(1)} copy-done((f32[64]{0:T(128)S(1)}, f32[64]{0:T(128)}, u32[]{:S(2)}) %copy-start.3) | copy-done | bytes 280
  1.3 0.0 copy-done.4
  1.3 0.0 copy-start
  1.3 0.8 %copy-done = f32[64,64]{1,0:T(8,128)S(1)} copy-done((f32[64,64]{1,0:T(8,128)S(1)}, f32[64,64]{1,0:T(8,128)}, u32[]{:S(2)}) %copy-start) | copy-done | bytes 16408
  2.1 0.0 copy-start.1
  2.1 0.8 %copy-done.1 = f32[64,64]{1,0:T(8,128)S(1)} copy-done((f32[64,64]{1,0:T(8,128)S(1)}, f32[64,64]{1,0:T(8,128)}, u32[]{:S(2)}) %copy-start.1) | copy-done | bytes 16408
  2.8 0.0 copy-start.2
  2.8 0.7 %copy-done.2 = f32[16,64]{1,0:T(8,128)S(1)} copy-done((f32[16,64]{1,0:T(8,128)S(1)}, f32[16,64]{1,0:T(8,128)}, u32[]{:S(2)}) %copy-start.2) | copy-done | bytes 4120
  3.5 27.0 %shard_map.68 = (f32[16,64]{1,0:T(8,128)S(1)}, f32[16,64]{1,0:T(8,128)S(1)}) custom-call(f32[64,64]{1,0:T(8,128)S(1)} %copy-done, f32[64,64]{1,0:T(8,128)S(1)} %copy-done.1, f32[1,64]{1,0:T(1,128)S(1)} %bitcast.2, f32[1,64]{1,0:T(1,128)S(1)} %bitcast.3, f32[16,64]{1,0:T(8,128)S(1)} %copy-done.2), custom_call_target="tpu_custom_call" | custom-call | tf_op jit(solution)/shard_map/pallas_call | solution.py:299
  30.6 0.6 %copy.9 = f32[16,64]{1,0:T(8,128)} copy(f32[16,64]{1,0:T(8,128)S(1)} %get-tuple-element.4) | data formatting | bytes 8192
  31.2 0.6 %copy.10 = f32[16,64]{1,0:T(8,128)} copy(f32[16,64]{1,0:T(8,128)S(1)} %get-tuple-element.5) | data formatting | bytes 8192
Async XLA Ops:
  0.6 0.7 %copy-start.3 = (f32[64]{0:T(128)S(1)}, f32[64]{0:T(128)}, u32[]{:S(2)}) copy-start(f32[64]{0:T(128)} %param.7) | copy-start | bytes 772
  0.6 0.7 %copy-start.4 = (f32[64]{0:T(128)S(1)}, f32[64]{0:T(128)}, u32[]{:S(2)}) copy-start(f32[64]{0:T(128)} %param.8) | copy-start | bytes 772
  1.3 0.8 %copy-start = (f32[64,64]{1,0:T(8,128)S(1)}, f32[64,64]{1,0:T(8,128)}, u32[]{:S(2)}) copy-start(f32[64,64]{1,0:T(8,128)} %train_ref.1) | copy-start | bytes 49156
  2.1 0.8 %copy-start.1 = (f32[64,64]{1,0:T(8,128)S(1)}, f32[64,64]{1,0:T(8,128)}, u32[]{:S(2)}) copy-start(f32[64,64]{1,0:T(8,128)} %cand_ref.1) | copy-start | bytes 49156
  2.8 0.7 %copy-start.2 = (f32[16,64]{1,0:T(8,128)S(1)}, f32[16,64]{1,0:T(8,128)}, u32[]{:S(2)}) copy-start(f32[16,64]{1,0:T(8,128)} %target_ref.1) | copy-start | bytes 12292

commit v2 on v1

v2 whole, which is shorter than its diff:
```python
import functools
import math

import jax
import jax.numpy as jnp
from jax import lax
from jax.experimental import pallas as pl
from jax.experimental.pallas import tpu as pltpu
from jax.sharding import PartitionSpec as P

MESH = pl.DeviceIdType.MESH
root_five = math.sqrt(5.0)
F32 = jnp.float32
BF16 = jnp.bfloat16


def lanes_of(rows):
    return lax.broadcasted_iota(jnp.int32, (rows, 128), 1)


def rounded(value):
    return value.astype(BF16).astype(F32)


def halves(doubled):
    high = rounded(doubled)
    return jnp.where(lanes_of(doubled.shape[0]) < 64, high, doubled - high).astype(BF16)


def whole(block):
    value = block.astype(F32)
    return value + pltpu.roll(value, 64, 1)


def doubled(value):
    return jnp.where(lanes_of(value.shape[0]) < 64, value, pltpu.roll(value, 64, 1))


def right_form(points):
    amount, dims = points.shape
    norm = jnp.sum(points * points, axis=1, keepdims=True)
    high = rounded(norm)
    middle = rounded(norm - high)
    low = rounded(norm - high - middle)
    lane = lanes_of(amount)
    right = jnp.concatenate([-2.0 * points, jnp.zeros((amount, 128 - dims), F32)], axis=1)
    for place, part in enumerate((high, middle, low)):
        right = jnp.where(lane == dims + place, part, right)
    return right.astype(BF16)


def right_operand(block):
    left_half = lanes_of(block.shape[0]) < 64
    value = block.astype(F32)
    return jnp.concatenate(
        [jnp.where(left_half, value, 1.0), jnp.where(left_half, 1.0, value)], axis=1
    ).astype(BF16)


def left_operand(block):
    left_half = lanes_of(block.shape[0]) < 64
    value = block.astype(F32)
    other = pltpu.roll(value, 64, 1)
    forms = []
    for here, there in ((value, other), (other, value)):
        high = rounded(there * there)
        square = here * here
        low = square - rounded(square)
        forms.append(
            jnp.concatenate(
                [jnp.where(left_half, here, high), jnp.where(left_half, low, 1.0)], axis=1
            )
        )
    return jnp.concatenate(forms, axis=0).astype(BF16)


def matern_split(left, right):
    dist = lax.dot_general(
        left, right, (((1,), (1,)), ((), ())), preferred_element_type=F32
    )
    dist = jnp.maximum(dist, 0.0)
    scaled = root_five * dist * lax.rsqrt(jnp.maximum(dist, 1e-30))
    kern = (1.0 + scaled + (5.0 / 3.0) * dist) * jnp.exp(-scaled)
    high = kern.astype(BF16)
    return high, (kern - high.astype(F32)).astype(BF16)


def pairs(slots):
    left_half = lanes_of(16) < 64
    return [
        jnp.where(left_half, slots[2 * h], slots[2 * h + 1]) for h in range(len(slots) // 2)
    ]


def rows_operand(slots):
    wide = jnp.concatenate(pairs(slots), axis=1)
    high = rounded(wide)
    return jnp.concatenate([high, wide - high], axis=0).astype(BF16)


def apply_tile(operand, high, low):
    both = jnp.dot(operand, high, preferred_element_type=F32)
    both += jnp.dot(operand, low, preferred_element_type=F32)
    return both[:16] + both[16:]


def column(value, lane_at):
    return jnp.sum(
        jnp.where(lanes_of(value.shape[0]) == lane_at, value, 0.0), axis=1, keepdims=True
    )


def kernel(
    rows, cols,
    train_hbm, cand_hbm, inv_hbm, noise_hbm, target_hbm,
    solution_ref, mean_ref,
    train_ref, cand_ref, inv_ref, noise_ref, target_ref,
    ibuf, jbuf, cbuf, train_hi, train_lo, cand_hi, cand_lo,
    psend, pbuf, vrow, vcol, wsend, wbuf, tcol, srow,
    in_sem, i_send, i_recv, j_send, j_recv, c_send, c_recv, p_send, p_recv,
    vr_send, vr_recv, vc_send, vc_recv, w_send, w_recv, t_send, t_recv, s_send, s_recv,
):
    loads = [
        pltpu.make_async_copy(src, dst, in_sem.at[n])
        for n, (src, dst) in enumerate(
            (
                (train_hbm, train_ref),
                (inv_hbm, inv_ref),
                (cand_hbm, cand_ref),
                (target_hbm, target_ref),
                (noise_hbm, noise_ref),
            )
        )
    ]
    for load in loads:
        load.start()
    a = lax.axis_index("row")
    b = lax.axis_index("col")
    row_peers = [lax.rem(a + k, rows) for k in range(1, rows)]
    col_peers = [lax.rem(b + k, cols) for k in range(1, cols)]
    order = [a] + [lax.rem(a + rows - k, rows) for k in range(1, rows)]
    group = 4
    groups = rows // group

    barrier = pltpu.get_barrier_semaphore()
    for p in row_peers:
        pl.semaphore_signal(barrier, inc=1, device_id=(p, b), device_id_type=MESH)
    for p in col_peers:
        pl.semaphore_signal(barrier, inc=1, device_id=(a, p), device_id_type=MESH)

    sent = []

    def to_row(src, buf, send, recv):
        for p in row_peers:
            copy = pltpu.make_async_remote_copy(
                src_ref=src, dst_ref=buf.at[a], send_sem=send.at[p], recv_sem=recv.at[a],
                device_id=(p, b), device_id_type=MESH,
            )
            copy.start()
            sent.append(copy)

    def to_col(src, buf, send, recv):
        for p in col_peers:
            copy = pltpu.make_async_remote_copy(
                src_ref=src(p), dst_ref=buf.at[b], send_sem=send.at[p], recv_sem=recv.at[b],
                device_id=(a, p), device_id_type=MESH,
            )
            copy.start()
            sent.append(copy)

    def arrived(buf, recv, peers):
        for p in peers:
            pltpu.make_async_remote_copy(
                src_ref=buf.at[p], dst_ref=buf.at[p], send_sem=recv.at[p], recv_sem=recv.at[p],
                device_id=(a, b), device_id_type=MESH,
            ).wait_recv()

    lane = lanes_of(16)
    left_half = lane < 64

    for load in loads:
        load.wait()
    own_points = train_ref.shape[1]
    points = jnp.concatenate([train_ref[...], cand_ref[...]], axis=1).T * inv_ref[...]
    points = rounded(points)
    own_train = points[:own_points]
    target = target_ref[...]
    target2 = jnp.concatenate([target, target], axis=1)
    target_block = halves(target2)
    noise = noise_ref[...]
    noise2 = jnp.concatenate([noise, noise], axis=1)
    ibuf[a, 0:32, :] = jnp.concatenate([own_train[:32], own_train[32:]], axis=1).astype(BF16)
    ibuf[a, 32:48, :] = target_block
    right = right_form(points)
    jbuf[b, 0:64, :] = right[:own_points]
    jbuf[b, 64:80, :] = target_block
    cbuf[b] = right[own_points:]

    pl.semaphore_wait(barrier, rows + cols - 2)
    to_row(ibuf.at[a], ibuf, i_send, i_recv)
    to_col(lambda p: jbuf.at[b], jbuf, j_send, j_recv)
    to_col(lambda p: cbuf.at[b], cbuf, c_send, c_recv)

    arrived(jbuf, j_recv, col_peers)
    right_train = right_operand(jbuf[:, 0:64, :].reshape(cols * 64, 128))

    def tile(slots, right, high_ref, low_ref, at):
        left = jnp.concatenate([left_operand(ibuf[order[k], 0:32, :]) for k in slots], axis=0)
        high, low = matern_split(left, right)
        high_ref[at : at + 64 * len(slots), :] = high
        low_ref[at : at + 64 * len(slots), :] = low

    def applied(slot_value, high_ref, low_ref):
        total = None
        for g in range(groups):
            span = slice(256 * g, 256 * g + 256)
            operand = rows_operand([slot_value(k) for k in range(group * g, group * g + group)])
            part = apply_tile(operand, high_ref[span, :], low_ref[span, :])
            total = part if total is None else total + part
        return total

    def targets_of(k):
        return whole(ibuf[order[k], 32:48, :])

    tile([0], right_train, train_hi, train_lo, 0)
    partial = None
    for g in range(groups):
        slots = list(range(max(1, group * g), group * g + group))
        arrived(ibuf, i_recv, [order[k] for k in slots])
        tile(slots, right_train, train_hi, train_lo, 64 * slots[0])
        span = slice(256 * g, 256 * g + 256)
        operand = rows_operand([targets_of(k) for k in range(group * g, group * g + group)])
        part = apply_tile(operand, train_hi[span, :], train_lo[span, :])
        partial = part if partial is None else partial + part

    def inner(wide, blocks):
        total = jnp.zeros((16, 128), F32)
        for h, block in enumerate(blocks):
            total += wide[:, 128 * h : 128 * h + 128] * block
        return jnp.sum(total, axis=1, keepdims=True)

    target_cols = [whole(jbuf[s, 64:80, :]) for s in range(cols)]
    own_bb = jnp.sum(target * target, axis=1, keepdims=True)
    own_bnb = jnp.sum(noise * target * target, axis=1, keepdims=True)
    scalars = jnp.where(
        lane == 64,
        inner(partial, pairs(target_cols)) + own_bnb,
        jnp.where(lane == 65, own_bb, 0.0),
    )
    for s in range(cols):
        piece = partial[:, 128 * (s // 2) : 128 * (s // 2) + 128]
        if s % 2:
            piece = pltpu.roll(piece, 64, 1)
        psend[s] = jnp.where(left_half, piece, scalars)
    to_col(lambda p: psend.at[p], pbuf, p_send, p_recv)

    arrived(cbuf, c_recv, col_peers)
    right_cand = right_operand(cbuf[...].reshape(cols * 64, 128))
    half = max(1, groups // 2)
    for g in range(half):
        tile(range(group * g, group * g + group), right_cand, cand_hi, cand_lo, 256 * g)

    arrived(pbuf, p_recv, col_peers)
    image = psend[b]
    for p in col_peers:
        image += pbuf[p]
    value = image + jnp.where(left_half, noise2 * target2, 0.0)
    vrow[a] = value
    vcol[b] = value
    to_row(vrow.at[a], vrow, vr_send, vr_recv)
    to_col(lambda p: vcol.at[b], vcol, vc_send, vc_recv)

    for g in range(half, groups):
        tile(range(group * g, group * g + group), right_cand, cand_hi, cand_lo, 256 * g)
    mean_b = applied(targets_of, cand_hi, cand_lo)

    arrived(vrow, vr_recv, row_peers)
    totals = vrow[0]
    for k in range(1, rows):
        totals += vrow[k]
    b_a_b = column(totals, 64)
    b_b = column(totals, 65)
    alpha = b_b / b_a_b

    def residual_of(k):
        return targets_of(k) - alpha * doubled(vrow[order[k]])

    image_r = applied(residual_of, train_hi, train_lo)
    arrived(vcol, vc_recv, col_peers)
    residual_cols = pairs([target_cols[s] - alpha * doubled(vcol[s]) for s in range(cols)])
    value_own = value[:, 0:64]
    residual_own = target - alpha * value_own
    square = residual_own * residual_own
    own_rar = inner(image_r, residual_cols) + jnp.sum(noise * square, axis=1, keepdims=True)
    own_rr = jnp.sum(square, axis=1, keepdims=True)
    own_vr = jnp.sum(value_own * residual_own, axis=1, keepdims=True)
    row_at = lax.broadcasted_iota(jnp.int32, (16, 128), 0)
    spread = jnp.where(
        lane == row_at,
        own_rar,
        jnp.where(lane == row_at + 16, own_rr, jnp.where(lane == row_at + 32, own_vr, 0.0)),
    )
    tcol[b] = jnp.broadcast_to(jnp.sum(spread, axis=0, keepdims=True), (8, 128))
    to_col(lambda p: tcol.at[b], tcol, t_send, t_recv)

    mean_r = applied(residual_of, cand_hi, cand_lo)
    for s in range(cols):
        at = 128 * (s // 2)
        first, second = mean_b[:, at : at + 128], mean_r[:, at : at + 128]
        if s % 2:
            first = pltpu.roll(first, 64, 1)
        else:
            second = pltpu.roll(second, 64, 1)
        wsend[s] = jnp.where(left_half, first, second)
    to_col(lambda p: wsend.at[p], wbuf, w_send, w_recv)

    arrived(tcol, t_recv, col_peers)
    totals = tcol[0]
    for s in range(1, cols):
        totals += tcol[s]
    srow[a] = totals
    to_row(srow.at[a], srow, s_send, s_recv)

    arrived(wbuf, w_recv, col_peers)
    means = wsend[b]
    for p in col_peers:
        means += wbuf[p]
    arrived(srow, s_recv, row_peers)
    totals = srow[0]
    for k in range(1, rows):
        totals += srow[k]
    totals = jnp.concatenate([totals, totals], axis=0)

    def unpacked(q):
        return jnp.sum(
            jnp.where(lane == row_at + 16 * q, totals, 0.0), axis=1, keepdims=True
        )

    r_a_r, fresh, v_r = unpacked(0), unpacked(1), unpacked(2)
    beta = fresh / b_b
    curve = r_a_r + 2.0 * beta * v_r + beta * beta * b_a_b
    alpha_two = fresh / curve
    share = alpha + alpha_two * beta
    solution_ref[...] = share * target + alpha_two * residual_own
    mean_ref[...] = share * means[:, 0:64] + alpha_two * means[:, 64:128]
    for copy in sent:
        copy.wait_send()


def per_device(rows, cols, train_points, cand_points, inv_length, noise, targets):
    vmem = pl.BlockSpec(memory_space=pltpu.VMEM)
    hbm = pl.BlockSpec(memory_space=pltpu.HBM)
    out = jax.ShapeDtypeStruct(targets.shape, F32)
    operands = (
        train_points, cand_points, inv_length.reshape(1, -1), noise.reshape(1, -1), targets
    )
    dma = pltpu.SemaphoreType.DMA
    width = cols * 64
    by_row, by_col = dma((rows,)), dma((cols,))
    kernel_tile = pltpu.VMEM((rows * 64, width), BF16)
    return pl.pallas_call(
        functools.partial(kernel, rows, cols),
        out_shape=(out, out),
        in_specs=[hbm] * 5,
        out_specs=(vmem, vmem),
        scratch_shapes=[pltpu.VMEM(operand.shape, F32) for operand in operands]
        + [
            pltpu.VMEM((rows, 48, 128), BF16),
            pltpu.VMEM((cols, 80, 128), BF16),
            pltpu.VMEM((cols, 64, 128), BF16),
            kernel_tile, kernel_tile, kernel_tile, kernel_tile,
            pltpu.VMEM((cols, 16, 128), F32),
            pltpu.VMEM((cols, 16, 128), F32),
            pltpu.VMEM((rows, 16, 128), F32),
            pltpu.VMEM((cols, 16, 128), F32),
            pltpu.VMEM((cols, 16, 128), F32),
            pltpu.VMEM((cols, 16, 128), F32),
            pltpu.VMEM((cols, 8, 128), F32),
            pltpu.VMEM((rows, 8, 128), F32),
            dma((5,)),
            by_row, by_row, by_col, by_col, by_col, by_col, by_col, by_col,
            by_row, by_row, by_col, by_col, by_col, by_col, by_col, by_col, by_row, by_row,
        ],
        compiler_params=pltpu.CompilerParams(
            collective_id=0, has_side_effects=True, vmem_limit_bytes=60 * 1024 * 1024
        ),
    )(*operands)


def solution(mesh):
    placed = (
        P(None, ("row", "col")),
        P(None, ("row", "col")),
        P(),
        P(("row", "col")),
        P(None, ("row", "col")),
    )
    return jax.shard_map(
        functools.partial(per_device, mesh.shape["row"], mesh.shape["col"]),
        mesh=mesh,
        in_specs=placed,
        out_specs=(P(None, ("row", "col")), P(None, ("row", "col"))),
        check_vma=False,
    )
```

time: 32.1 us -> 29.3 us (0.913)
  local copies, waits for them, and re-layouts: 4.07 us -> 1.9 us
  Pallas kernels: 27 us -> 26.5 us
    unnamed x12 -> x4, local copies, waits for them, and re-layouts: 4.07 us -> 1.9 us
    pallas_call x1, Pallas kernels: 27 us -> 26.5 us  [per_device(): pl.pallas_call(functools.partial(kernel, rows, cols), out_shape=(out, out...]
where the time goes in v2:
time: 29.3 us; the launch traced here: 29.1 us
  Pallas kernels  26.5 us (90%)
  local copies, waits for them, and re-layouts  1.9 us (6%)
  between operations  0.65 us (2%)
    pallas_call x1, Pallas kernels, per_device(): pl.pallas_call(functools.partial(kernel, rows, cols), out_shape=(out, out...  26.5 us
    unnamed x4, local copies, waits for them, and re-layouts  1.9 us

profile of v2, /device:TPU:0, one launch (start us, length us, event | category | flops | bytes accessed | tf_op | source)
XLA Modules:
  0.0 29.1 jit_solution(6464500859344812280)
XLA Ops:
  0.6 26.5 %shard_map.68 = (f32[16,64]{1,0:T(8,128)}, f32[16,64]{1,0:T(8,128)}) custom-call(f32[64,64]{1,0:T(8,128)} %train_hbm.1, f32[64,64]{1,0:T(8,128)} %cand_hbm.1, f32[1,64]{1,0:T(1,128)} %bitcast.2, f32[1,64]{1,0:T(1,128)} %bitcast.3, f32[16,64]{1,0:T(8,128)} %target_hbm.1), custom_call_target="tpu_custom_call" | custom-call | tf_op jit(solution)/shard_map/pallas_call | solution.py:361
  27.1 0.0 copy-start
  27.1 1.3 %copy.9 = f32[16,64]{1,0:T(8,128)} copy(f32[16,64]{1,0:T(8,128)} %get-tuple-element.4) | data formatting | bytes 8192
  28.5 0.0 copy-done
  28.5 0.6 %copy.10 = f32[16,64]{1,0:T(8,128)} copy(f32[16,64]{1,0:T(8,128)S(1)} %copy-done) | data formatting | bytes 8192
Async XLA Ops:
  27.1 1.3 %copy-start = (f32[16,64]{1,0:T(8,128)S(1)}, f32[16,64]{1,0:T(8,128)}, u32[]{:S(2)}) copy-start(f32[16,64]{1,0:T(8,128)} %get-tuple-element.5) | copy-start | bytes 12292

commit v3 on v2

--- a/solution.py
+++ b/solution.py
@@ -116,9 +116,9 @@
     solution_ref, mean_ref,
     train_ref, cand_ref, inv_ref, noise_ref, target_ref,
     ibuf, jbuf, cbuf, train_hi, train_lo, cand_hi, cand_lo,
-    psend, pbuf, vrow, vcol, wsend, wbuf, tcol, srow,
+    psend, pbuf, vrow, vcol, wsend, wbuf, total_ref,
     in_sem, i_send, i_recv, j_send, j_recv, c_send, c_recv, p_send, p_recv,
-    vr_send, vr_recv, vc_send, vc_recv, w_send, w_recv, t_send, t_recv, s_send, s_recv,
+    vr_send, vr_recv, vc_send, vc_recv, w_send, w_recv, s_send, s_recv,
 ):
     loads = [
         pltpu.make_async_copy(src, dst, in_sem.at[n])
@@ -143,37 +143,54 @@
     groups = rows // group
 
     barrier = pltpu.get_barrier_semaphore()
-    for p in row_peers:
-        pl.semaphore_signal(barrier, inc=1, device_id=(p, b), device_id_type=MESH)
-    for p in col_peers:
-        pl.semaphore_signal(barrier, inc=1, device_id=(a, p), device_id_type=MESH)
+    devices = rows * cols
+    me = a * cols + b
+
+    def each_other(act):
+        def step(k, carry):
+            other = lax.rem(me + k, devices)
+            act((lax.div(other, cols), lax.rem(other, cols)))
+            return carry
+
+        if devices <= 64:
+            for k in range(1, devices):
+                step(k, 0)
+        else:
+            lax.fori_loop(1, devices, step, 0)
+
+    each_other(
+        lambda device: pl.semaphore_signal(
+            barrier, inc=1, device_id=device, device_id_type=MESH
+        )
+    )
 
     sent = []
+
+    def start(src, dst, send, recv, device):
+        pltpu.make_async_remote_copy(
+            src_ref=src, dst_ref=dst, send_sem=send, recv_sem=recv,
+            device_id=device, device_id_type=MESH,
+        ).start()
+
+    def blocks(buf, amount, sem):
+        span = buf.at[pl.ds(0, amount)]
+        return pltpu.make_async_remote_copy(
+            src_ref=span, dst_ref=span, send_sem=sem, recv_sem=sem,
+            device_id=(a, b), device_id_type=MESH,
+        )
 
     def to_row(src, buf, send, recv):
         for p in row_peers:
-            copy = pltpu.make_async_remote_copy(
-                src_ref=src, dst_ref=buf.at[a], send_sem=send.at[p], recv_sem=recv.at[a],
-                device_id=(p, b), device_id_type=MESH,
-            )
-            copy.start()
-            sent.append(copy)
+            start(src, buf.at[a], send, recv, (p, b))
+        sent.append(blocks(buf, rows - 1, send))
 
     def to_col(src, buf, send, recv):
         for p in col_peers:
-            copy = pltpu.make_async_remote_copy(
-                src_ref=src(p), dst_ref=buf.at[b], send_sem=send.at[p], recv_sem=recv.at[b],
-                device_id=(a, p), device_id_type=MESH,
-            )
-            copy.start()
-            sent.append(copy)
-
-    def arrived(buf, recv, peers):
-        for p in peers:
-            pltpu.make_async_remote_copy(
-                src_ref=buf.at[p], dst_ref=buf.at[p], send_sem=recv.at[p], recv_sem=recv.at[p],
-                device_id=(a, b), device_id_type=MESH,
-            ).wait_recv()
+            start(src(p), buf.at[b], send, recv, (a, p))
+        sent.append(blocks(buf, cols - 1, send))
+
+    def all_arrived(buf, recv):
+        blocks(buf, buf.shape[0] - 1, recv).wait_recv()
 
     lane = lanes_of(16)
     left_half = lane < 64
@@ -196,12 +213,14 @@
     jbuf[b, 64:80, :] = target_block
     cbuf[b] = right[own_points:]
 
-    pl.semaphore_wait(barrier, rows + cols - 2)
-    to_row(ibuf.at[a], ibuf, i_send, i_recv)
+    pl.semaphore_wait(barrier, devices - 1)
+    for p in row_peers:
+        start(ibuf.at[a], ibuf.at[a], i_send, i_recv.at[a], (p, b))
+    sent.append(blocks(ibuf, rows - 1, i_send))
     to_col(lambda p: jbuf.at[b], jbuf, j_send, j_recv)
     to_col(lambda p: cbuf.at[b], cbuf, c_send, c_recv)
 
-    arrived(jbuf, j_recv, col_peers)
+    all_arrived(jbuf, j_recv)
     right_train = right_operand(jbuf[:, 0:64, :].reshape(cols * 64, 128))
 
     def tile(slots, right, high_ref, low_ref, at):
@@ -226,7 +245,12 @@
     partial = None
     for g in range(groups):
         slots = list(range(max(1, group * g), group * g + group))
-        arrived(ibuf, i_recv, [order[k] for k in slots])
+        for k in slots:
+            p = order[k]
+            pltpu.make_async_remote_copy(
+                src_ref=ibuf.at[p], dst_ref=ibuf.at[p], send_sem=i_send, recv_sem=i_recv.at[p],
+                device_id=(a, b), device_id_type=MESH,
+            ).wait_recv()
         tile(slots, right_train, train_hi, train_lo, 64 * slots[0])
         span = slice(256 * g, 256 * g + 256)
         operand = rows_operand([targets_of(k) for k in range(group * g, group * g + group)])
@@ -254,13 +278,13 @@
         psend[s] = jnp.where(left_half, piece, scalars)
     to_col(lambda p: psend.at[p], pbuf, p_send, p_recv)
 
-    arrived(cbuf, c_recv, col_peers)
+    all_arrived(cbuf, c_recv)
     right_cand = right_operand(cbuf[...].reshape(cols * 64, 128))
     half = max(1, groups // 2)
     for g in range(half):
         tile(range(group * g, group * g + group), right_cand, cand_hi, cand_lo, 256 * g)
 
-    arrived(pbuf, p_recv, col_peers)
+    all_arrived(pbuf, p_recv)
     image = psend[b]
     for p in col_peers:
         image += pbuf[p]
@@ -274,7 +298,7 @@
         tile(range(group * g, group * g + group), right_cand, cand_hi, cand_lo, 256 * g)
     mean_b = applied(targets_of, cand_hi, cand_lo)
 
-    arrived(vrow, vr_recv, row_peers)
+    all_arrived(vrow, vr_recv)
     totals = vrow[0]
     for k in range(1, rows):
         totals += vrow[k]
@@ -286,7 +310,7 @@
         return targets_of(k) - alpha * doubled(vrow[order[k]])
 
     image_r = applied(residual_of, train_hi, train_lo)
-    arrived(vcol, vc_recv, col_peers)
+    all_arrived(vcol, vc_recv)
     residual_cols = pairs([target_cols[s] - alpha * doubled(vcol[s]) for s in range(cols)])
     value_own = value[:, 0:64]
     residual_own = target - alpha * value_own
@@ -300,8 +324,11 @@
         own_rar,
         jnp.where(lane == row_at + 16, own_rr, jnp.where(lane == row_at + 32, own_vr, 0.0)),
     )
-    tcol[b] = jnp.broadcast_to(jnp.sum(spread, axis=0, keepdims=True), (8, 128))
-    to_col(lambda p: tcol.at[b], tcol, t_send, t_recv)
+    total_ref[me] = jnp.sum(spread, axis=0, keepdims=True)
+    each_other(
+        lambda device: start(total_ref.at[me], total_ref.at[me], s_send, s_recv, device)
+    )
+    sent.append(blocks(total_ref, devices - 1, s_send))
 
     mean_r = applied(residual_of, cand_hi, cand_lo)
     for s in range(cols):
@@ -314,22 +341,12 @@
         wsend[s] = jnp.where(left_half, first, second)
     to_col(lambda p: wsend.at[p], wbuf, w_send, w_recv)
 
-    arrived(tcol, t_recv, col_peers)
-    totals = tcol[0]
-    for s in range(1, cols):
-        totals += tcol[s]
-    srow[a] = totals
-    to_row(srow.at[a], srow, s_send, s_recv)
-
-    arrived(wbuf, w_recv, col_peers)
+    all_arrived(wbuf, w_recv)
     means = wsend[b]
     for p in col_peers:
         means += wbuf[p]
-    arrived(srow, s_recv, row_peers)
-    totals = srow[0]
-    for k in range(1, rows):
-        totals += srow[k]
-    totals = jnp.concatenate([totals, totals], axis=0)
+    all_arrived(total_ref, s_recv)
+    totals = jnp.sum(total_ref[...], axis=0)
 
     def unpacked(q):
         return jnp.sum(
@@ -350,13 +367,12 @@
 def per_device(rows, cols, train_points, cand_points, inv_length, noise, targets):
     vmem = pl.BlockSpec(memory_space=pltpu.VMEM)
     hbm = pl.BlockSpec(memory_space=pltpu.HBM)
-    out = jax.ShapeDtypeStruct(targets.shape, F32)
+    out = pltpu.VMEM(targets.shape, F32)
     operands = (
         train_points, cand_points, inv_length.reshape(1, -1), noise.reshape(1, -1), targets
     )
     dma = pltpu.SemaphoreType.DMA
     width = cols * 64
-    by_row, by_col = dma((rows,)), dma((cols,))
     kernel_tile = pltpu.VMEM((rows * 64, width), BF16)
     return pl.pallas_call(
         functools.partial(kernel, rows, cols),
@@ -375,12 +391,10 @@
             pltpu.VMEM((cols, 16, 128), F32),
             pltpu.VMEM((cols, 16, 128), F32),
             pltpu.VMEM((cols, 16, 128), F32),
-            pltpu.VMEM((cols, 8, 128), F32),
-            pltpu.VMEM((rows, 8, 128), F32),
-            dma((5,)),
-            by_row, by_row, by_col, by_col, by_col, by_col, by_col, by_col,
-            by_row, by_row, by_col, by_col, by_col, by_col, by_col, by_col, by_row, by_row,
-        ],
+            pltpu.VMEM((rows * cols, 1, 128), F32),
+            dma((5,)), dma, dma((rows,)),
+        ]
+        + [dma] * 14,
         compiler_params=pltpu.CompilerParams(
             collective_id=0, has_side_effects=True, vmem_limit_bytes=60 * 1024 * 1024
         ),

time: 29.3 us -> 25.4 us (0.87)
  Pallas kernels: 26.5 us -> 23.4 us
  local copies, waits for them, and re-layouts: 1.9 us -> 1.2 us
    pallas_call x1, Pallas kernels: 26.5 us -> 23.4 us  [per_device(): pl.pallas_call(functools.partial(kernel, rows, cols), out_shape=(out, out...]
    unnamed x4 -> x2, local copies, waits for them, and re-layouts: 1.9 us -> 1.2 us
where the time goes in v3:
time: 25.4 us; the launch traced here: 25.2 us
  Pallas kernels  23.4 us (92%)
  local copies, waits for them, and re-layouts  1.2 us (5%)
  between operations  0.64 us (3%)
    pallas_call x1, Pallas kernels, per_device(): pl.pallas_call(functools.partial(kernel, rows, cols), out_shape=(out, out...  23.4 us
    unnamed x2, local copies, waits for them, and re-layouts  1.2 us

profile of v3, /device:TPU:0, one launch (start us, length us, event | category | flops | bytes accessed | tf_op | source)
XLA Modules:
  0.0 25.2 jit_solution(17059344785526654451)
XLA Ops:
  0.6 23.4 %shard_map.68 = (f32[16,64]{1,0:T(8,128)S(1)}, f32[16,64]{1,0:T(8,128)S(1)}) custom-call(f32[64,64]{1,0:T(8,128)} %train_hbm.1, f32[64,64]{1,0:T(8,128)} %cand_hbm.1, f32[1,64]{1,0:T(1,128)} %bitcast.2, f32[1,64]{1,0:T(1,128)} %bitcast.3, f32[16,64]{1,0:T(8,128)} %target_hbm.1), custom_call_target="tpu_custom_call" | custom-call | tf_op jit(solution)/shard_map/pallas_call | solution.py:377
  24.0 0.6 %copy.9 = f32[16,64]{1,0:T(8,128)} copy(f32[16,64]{1,0:T(8,128)S(1)} %get-tuple-element.2) | data formatting | bytes 8192
  24.6 0.6 %copy.10 = f32[16,64]{1,0:T(8,128)} copy(f32[16,64]{1,0:T(8,128)S(1)} %get-tuple-element.3) | data formatting | bytes 8192

commit v4 on v0

v4 whole, which is shorter than its diff:
```python
import functools
import math

import jax
import jax.numpy as jnp
from jax import lax
from jax.experimental import pallas as pl
from jax.experimental.pallas import tpu as pltpu
from jax.sharding import PartitionSpec as P

MESH = pl.DeviceIdType.MESH
root_five = math.sqrt(5.0)
F32 = jnp.float32
BF16 = jnp.bfloat16


def in_left(rows):
    return lax.broadcasted_iota(jnp.int32, (rows, 128), 1) < 64


def turned(value):
    return pltpu.roll(value, 64, 1)


def rounded(value):
    return value.astype(BF16).astype(F32)


def halves(doubled):
    high = rounded(doubled)
    return jnp.where(in_left(doubled.shape[0]), high, doubled - high).astype(BF16)


def whole(block):
    value = block.astype(F32)
    return value + turned(value)


def packed(wide, second):
    top, bottom = wide[0:8], wide[8:16]
    if second:
        return jnp.where(in_left(8), turned(top), bottom)
    return jnp.where(in_left(8), top, turned(bottom))


def unpacked(first, second):
    left = in_left(8)
    return jnp.concatenate(
        [jnp.where(left, first, turned(second)), jnp.where(left, turned(first), second)], axis=0
    )


def both_halves(block):
    value = block.astype(F32)
    other = turned(value)
    return (value, other), (other, value)


def squares(value):
    square = value * value
    high = rounded(square)
    return high, square - high


def left_operand(block):
    left = in_left(block.shape[0])
    forms = []
    for here, there in both_halves(block):
        high, low = squares(there)[0], squares(here)[1]
        forms.append(
            jnp.concatenate([jnp.where(left, here, high), jnp.where(left, low, 0.0)], axis=1)
        )
    return jnp.concatenate(forms, axis=0).astype(BF16)


def right_operand(blocks):
    forms, square_forms = [], []
    for block in blocks:
        left = in_left(block.shape[0])
        for here, there in both_halves(block):
            forms.append(
                jnp.concatenate(
                    [jnp.where(left, -2.0 * here, 1.0), jnp.where(left, 1.0, 0.0)], axis=1
                )
            )
            square_forms.append(jnp.where(left, squares(here)[0], squares(there)[1]))
    operand = jnp.concatenate(forms, axis=0).astype(BF16)
    summed = lax.dot_general(
        jnp.ones((16, 128), BF16),
        jnp.concatenate(square_forms, axis=0).astype(BF16),
        (((1,), (1,)), ((), ())),
        preferred_element_type=F32,
    )
    return operand, summed[0:1]


def matern_split(left, right, right_norm):
    dist = lax.dot_general(
        left, right, (((1,), (1,)), ((), ())), preferred_element_type=F32
    )
    dist = jnp.maximum(dist + right_norm, 0.0)
    scaled = root_five * dist * lax.rsqrt(jnp.maximum(dist, 1e-30))
    kern = (1.0 + scaled + (5.0 / 3.0) * dist) * jnp.exp(-scaled)
    high = kern.astype(BF16)
    return high, (kern - high.astype(F32)).astype(BF16)


def pairs(slots):
    left = in_left(16)
    return [jnp.where(left, slots[2 * h], slots[2 * h + 1]) for h in range(len(slots) // 2)]


def unpacked_pairs(slots):
    return [unpacked(slots[2 * h], slots[2 * h + 1]) for h in range(len(slots) // 2)]


def applied(blocks, high_ref, low_ref):
    total = None
    for at in range(0, len(blocks), 2):
        wide = jnp.concatenate(blocks[at : at + 2], axis=1)
        high = rounded(wide)
        operand = jnp.concatenate([high, wide - high], axis=0).astype(BF16)
        span = slice(128 * at, 128 * at + wide.shape[1])
        part = jnp.dot(operand, high_ref[span, :], preferred_element_type=F32)
        part += jnp.dot(operand, low_ref[span, :], preferred_element_type=F32)
        total = part if total is None else total + part
    return total[:16] + total[16:]


def kernel(
    rows, cols,
    train_hbm, cand_hbm, inv_hbm, noise_hbm, target_hbm,
    solution_ref, mean_ref,
    train_ref, cand_ref, inv_ref, noise_ref, target_ref,
    lbuf, pbuf, cbuf, train_hi, train_lo, cand_hi, cand_lo,
    image_send, image_buf, vline, vplane, wsend, wbuf, first_ref, last_ref,
    in_sem, l_recv,
    l_send, p_send, p_recv, c_send, c_recv, image_out, image_in,
    vl_send, vl_recv, vp_send, vp_recv, w_send, w_recv,
    first_send, first_recv, last_send, last_recv,
):
    loads = [
        pltpu.make_async_copy(src, dst, in_sem.at[n])
        for n, (src, dst) in enumerate(
            (
                (train_hbm, train_ref),
                (inv_hbm, inv_ref),
                (target_hbm, target_ref),
                (cand_hbm, cand_ref),
                (noise_hbm, noise_ref),
            )
        )
    ]
    for load in loads:
        load.start()
    a = lax.axis_index("row")
    b = lax.axis_index("col")
    devices = rows * cols
    me = a * cols + b
    z, core = lax.div(a, 2), lax.rem(a, 2)
    line, plane = rows // 2, 2 * cols
    spot = core * cols + b
    line_peers = [lax.rem(z + k, line) for k in range(1, line)]
    plane_peers = [lax.rem(spot + k, plane) for k in range(1, plane)]
    order = [z] + [lax.rem(z + line - k, line) for k in range(1, line)]

    def each_other(act):
        def step(k, carry):
            other = lax.rem(me + k, devices)
            act((lax.div(other, cols), lax.rem(other, cols)))
            return carry

        if devices <= 64:
            for k in range(1, devices):
                step(k, 0)
        else:
            lax.fori_loop(1, devices, step, 0)

    barrier = pltpu.get_barrier_semaphore()
    each_other(
        lambda device: pl.semaphore_signal(
            barrier, inc=1, device_id=device, device_id_type=MESH
        )
    )

    sent = []

    def start(src, dst, send, recv, device):
        pltpu.make_async_remote_copy(
            src_ref=src, dst_ref=dst, send_sem=send, recv_sem=recv,
            device_id=device, device_id_type=MESH,
        ).start()

    def blocks(buf, amount, sem):
        span = buf.at[pl.ds(0, amount)]
        return pltpu.make_async_remote_copy(
            src_ref=span, dst_ref=span, send_sem=sem, recv_sem=sem,
            device_id=(a, b), device_id_type=MESH,
        )

    def to_line(src, buf, send, recv):
        for p in line_peers:
            start(src, buf.at[z], send, recv, (2 * p + core, b))
        sent.append(blocks(buf, line - 1, send))

    def to_plane(src, buf, send, recv):
        for p in plane_peers:
            device = (2 * z + lax.div(p, cols), lax.rem(p, cols))
            start(src(p), buf.at[spot], send, recv, device)
        sent.append(blocks(buf, plane - 1, send))

    def to_all(buf, send, recv):
        each_other(lambda device: start(buf.at[me], buf.at[me], send, recv, device))
        sent.append(blocks(buf, devices - 1, send))

    def arrived(buf, recv):
        blocks(buf, buf.shape[0] - 1, recv).wait_recv()

    lane = lax.broadcasted_iota(jnp.int32, (16, 128), 1)
    row_at = lax.broadcasted_iota(jnp.int32, (16, 128), 0)
    left16 = lane < 64

    def points_of(ref):
        scaled = rounded(ref[...].T * inv_ref[...])
        return jnp.concatenate([scaled[:32], scaled[32:]], axis=1).astype(BF16)

    def spread(columns):
        total = jnp.zeros((16, 128), F32)
        for q, one in enumerate(columns):
            total = jnp.where(lane == row_at + 16 * q, one, total)
        return jnp.sum(total, axis=0, keepdims=True)

    def gathered(ref, amount):
        total = jnp.sum(ref[...], axis=0)
        return [
            jnp.sum(jnp.where(lane == row_at + 16 * q, total, 0.0), axis=1, keepdims=True)
            for q in range(amount)
        ]

    def inner(wide, lane_blocks):
        total = jnp.zeros((16, 128), F32)
        for h, block in enumerate(lane_blocks):
            total += wide[:, 128 * h : 128 * h + 128] * block
        return jnp.sum(total, axis=1, keepdims=True)

    for load in loads[:3]:
        load.wait()
    target = target_ref[...]
    target2 = jnp.concatenate([target, target], axis=1)
    target_block = halves(target2)
    own_train = points_of(train_ref)
    lbuf[z, 0:32, :] = own_train
    lbuf[z, 32:48, :] = target_block
    pbuf[spot, 0:32, :] = own_train
    pbuf[spot, 32:48, :] = target_block
    pl.semaphore_wait(barrier, devices - 1)
    for p in line_peers:
        start(lbuf.at[z], lbuf.at[z], l_send, l_recv.at[z], (2 * p + core, b))
    sent.append(blocks(lbuf, line - 1, l_send))
    to_plane(lambda p: pbuf.at[spot], pbuf, p_send, p_recv)
    loads[3].wait()
    cbuf[spot] = points_of(cand_ref)
    to_plane(lambda p: cbuf.at[spot], cbuf, c_send, c_recv)
    loads[4].wait()
    noise = noise_ref[...]
    noise2 = jnp.concatenate([noise, noise], axis=1)

    def tile(slots, right, right_norm, high_ref, low_ref):
        left = jnp.concatenate([left_operand(lbuf[order[k], 0:32, :]) for k in slots], axis=0)
        span = slice(64 * slots[0], 64 * slots[0] + 64 * len(slots))
        high_ref[span, :], low_ref[span, :] = matern_split(left, right, right_norm)

    arrived(pbuf, p_recv)
    right_train, train_norm = right_operand([pbuf[s, 0:32, :] for s in range(plane)])
    tile([0], right_train, train_norm, train_hi, train_lo)
    for at in range(0, line, 4):
        slots = list(range(max(1, at), min(line, at + 4)))
        for k in slots:
            p = order[k]
            pltpu.make_async_remote_copy(
                src_ref=lbuf.at[p], dst_ref=lbuf.at[p], send_sem=l_send, recv_sem=l_recv.at[p],
                device_id=(a, b), device_id_type=MESH,
            ).wait_recv()
        tile(slots, right_train, train_norm, train_hi, train_lo)
    target_line = pairs([whole(lbuf[order[k], 32:48, :]) for k in range(line)])
    partial = applied(target_line, train_hi, train_lo)
    for s in range(plane):
        image_send[s] = packed(partial[:, 128 * (s // 2) : 128 * (s // 2) + 128], s % 2)
    to_plane(lambda p: image_send.at[p], image_buf, image_out, image_in)

    target_plane = pairs([whole(pbuf[s, 32:48, :]) for s in range(plane)])
    own_bb = jnp.sum(target * target, axis=1, keepdims=True)
    own_bnb = jnp.sum(noise * target * target, axis=1, keepdims=True)
    first_ref[me] = spread([inner(partial, target_plane) + own_bnb, own_bb])
    to_all(first_ref, first_send, first_recv)

    arrived(cbuf, c_recv)
    right_cand, cand_norm = right_operand([cbuf[s] for s in range(plane)])
    chunk = min(4, line // 2)
    chunks = [list(range(at, at + chunk)) for at in range(0, line, chunk)]
    half = len(chunks) // 2
    for slots in chunks[:half]:
        tile(slots, right_cand, cand_norm, cand_hi, cand_lo)

    arrived(image_buf, image_in)
    image = image_send[spot]
    for p in plane_peers:
        image += image_buf[p]
    left8 = in_left(8)
    target_packed = jnp.where(left8, target2[0:8], target2[8:16])
    value = image + noise2 * target_packed
    vline[z] = value
    vplane[spot] = value
    to_line(vline.at[z], vline, vl_send, vl_recv)
    to_plane(lambda p: vplane.at[spot], vplane, vp_send, vp_recv)

    for slots in chunks[half:]:
        tile(slots, right_cand, cand_norm, cand_hi, cand_lo)
    mean_b = applied(target_line, cand_hi, cand_lo)

    arrived(first_ref, first_recv)
    b_a_b, b_b = gathered(first_ref, 2)
    alpha = b_b / b_a_b

    def residuals(target_blocks, slots):
        return [
            block - alpha * values for block, values in zip(target_blocks, unpacked_pairs(slots))
        ]

    arrived(vline, vl_recv)
    residual_line = residuals(target_line, [vline[order[k]] for k in range(line)])
    image_r = applied(residual_line, train_hi, train_lo)
    arrived(vplane, vp_recv)
    residual_plane = residuals(target_plane, [vplane[s] for s in range(plane)])
    value_own = unpacked(value, value)[:, 0:64]
    residual_own = target - alpha * value_own
    square = residual_own * residual_own
    own_rar = inner(image_r, residual_plane) + jnp.sum(noise * square, axis=1, keepdims=True)
    own_rr = jnp.sum(square, axis=1, keepdims=True)
    own_vr = jnp.sum(value_own * residual_own, axis=1, keepdims=True)
    last_ref[me] = spread([own_rar, own_rr, own_vr])
    to_all(last_ref, last_send, last_recv)

    mean_r = applied(residual_line, cand_hi, cand_lo)
    for s in range(plane):
        at = 128 * (s // 2)
        first, second = mean_b[:, at : at + 128], mean_r[:, at : at + 128]
        if s % 2:
            first = turned(first)
        else:
            second = turned(second)
        wsend[s] = jnp.where(left16, first, second)
    to_plane(lambda p: wsend.at[p], wbuf, w_send, w_recv)

    arrived(wbuf, w_recv)
    means = wsend[spot]
    for p in plane_peers:
        means += wbuf[p]
    arrived(last_ref, last_recv)
    r_a_r, fresh, v_r = gathered(last_ref, 3)
    beta = fresh / b_b
    curve = r_a_r + 2.0 * beta * v_r + beta * beta * b_a_b
    alpha_two = fresh / curve
    share = alpha + alpha_two * beta
    solution_ref[...] = share * target + alpha_two * residual_own
    mean_ref[...] = share * means[:, 0:64] + alpha_two * means[:, 64:128]
    for copy in sent:
        copy.wait_send()


def per_device(rows, cols, train_points, cand_points, inv_length, noise, targets):
    vmem = pl.BlockSpec(memory_space=pltpu.VMEM)
    hbm = pl.BlockSpec(memory_space=pltpu.HBM)
    out = pltpu.VMEM(targets.shape, F32)
    operands = (
        train_points, cand_points, inv_length.reshape(1, -1), noise.reshape(1, -1), targets
    )
    dma = pltpu.SemaphoreType.DMA
    line, plane = rows // 2, 2 * cols
    kernel_tile = pltpu.VMEM((line * 64, plane * 64), BF16)
    return pl.pallas_call(
        functools.partial(kernel, rows, cols),
        out_shape=(out, out),
        in_specs=[hbm] * 5,
        out_specs=(vmem, vmem),
        scratch_shapes=[pltpu.VMEM(operand.shape, F32) for operand in operands]
        + [
            pltpu.VMEM((line, 48, 128), BF16),
            pltpu.VMEM((plane, 48, 128), BF16),
            pltpu.VMEM((plane, 32, 128), BF16),
            kernel_tile, kernel_tile, kernel_tile, kernel_tile,
            pltpu.VMEM((plane, 8, 128), F32),
            pltpu.VMEM((plane, 8, 128), F32),
            pltpu.VMEM((line, 8, 128), F32),
            pltpu.VMEM((plane, 8, 128), F32),
            pltpu.VMEM((plane, 16, 128), F32),
            pltpu.VMEM((plane, 16, 128), F32),
            pltpu.VMEM((rows * cols, 1, 128), F32),
            pltpu.VMEM((rows * cols, 1, 128), F32),
            dma((5,)), dma((line,)),
        ]
        + [dma] * 17,
        compiler_params=pltpu.CompilerParams(
            collective_id=0, has_side_effects=True, vmem_limit_bytes=60 * 1024 * 1024
        ),
    )(*operands)


def solution(mesh):
    placed = (
        P(None, ("row", "col")),
        P(None, ("row", "col")),
        P(),
        P(("row", "col")),
        P(None, ("row", "col")),
    )
    return jax.shard_map(
        functools.partial(per_device, mesh.shape["row"], mesh.shape["col"]),
        mesh=mesh,
        in_specs=placed,
        out_specs=(P(None, ("row", "col")), P(None, ("row", "col"))),
        check_vma=False,
    )
```

time: 292 us -> 25 us (0.09)
  blocking collectives: 193 us -> 0 us
  waiting for transfers between devices: 73.2 us -> 0 us
  Pallas kernels: 0 us -> 23 us
  between operations: 13.8 us -> 0.64 us
  local copies, waits for them, and re-layouts: 6.18 us -> 1.2 us
  matrix products: 4.49 us -> 0 us
    psum x3 -> x0, blocking collectives: 118 us -> none  [the longest x2 78.6 us: squares(): return lax.psum(jnp.sum(residual * residual, axis=1), ('row', 'col'))]
    all_gather x6 -> x0, blocking collectives: 74.8 us -> none  [the longest x2 27.9 us: per_device(): lax.all_gather(direction, 'row', axis=1, tiled=True)]
    unnamed x6 -> x0, waiting for transfers between devices: 73.2 us -> none
    pallas_call x0 -> x1, Pallas kernels: none -> 23 us  [per_device(): pl.pallas_call(functools.partial(kernel, rows, cols), out_shape=(out, out...]
    unnamed x19 -> x2, local copies, waits for them, and re-layouts: 6.11 us -> 1.2 us
    unnamed x2 -> x0, matrix products: 3.4 us -> none
  transfers between devices with their start and end apart: 3 -> 0, of which waited for: 3 -> 0; matrix products, arithmetic and copies ran while one was open for 0% -> 0% of each run, Pallas kernels for 0% -> 0%
where the time goes in v4:
time: 25 us; the launch traced here: 24.8 us
  Pallas kernels  23 us (92%)
  local copies, waits for them, and re-layouts  1.2 us (5%)
  between operations  0.64 us (3%)
    pallas_call x1, Pallas kernels, per_device(): pl.pallas_call(functools.partial(kernel, rows, cols), out_shape=(out, out...  23 us
    unnamed x2, local copies, waits for them, and re-layouts  1.2 us

profile of v4, /device:TPU:0, one launch (start us, length us, event | category | flops | bytes accessed | tf_op | source)
XLA Modules:
  0.0 24.8 jit_solution(15013188360035754806)
XLA Ops:
  0.6 23.0 %shard_map.68 = (f32[16,64]{1,0:T(8,128)S(1)}, f32[16,64]{1,0:T(8,128)S(1)}) custom-call(f32[64,64]{1,0:T(8,128)} %train_hbm.1, f32[64,64]{1,0:T(8,128)} %cand_hbm.1, f32[1,64]{1,0:T(1,128)} %bitcast.2, f32[1,64]{1,0:T(1,128)} %bitcast.3, f32[16,64]{1,0:T(8,128)} %target_hbm.1), custom_call_target="tpu_custom_call" | custom-call | tf_op jit(solution)/shard_map/pallas_call | solution.py:381
  23.6 0.6 %copy.9 = f32[16,64]{1,0:T(8,128)} copy(f32[16,64]{1,0:T(8,128)S(1)} %get-tuple-element.2) | data formatting | bytes 8192
  24.2 0.6 %copy.10 = f32[16,64]{1,0:T(8,128)} copy(f32[16,64]{1,0:T(8,128)S(1)} %get-tuple-element.3) | data formatting | bytes 8192

commit v5 on v4

--- a/solution.py
+++ b/solution.py
@@ -94,15 +94,17 @@
     return operand, summed[0:1]
 
 
-def matern_split(left, right, right_norm):
-    dist = lax.dot_general(
+def matern_split(left, right, right_norm, high_ref, low_ref, at):
+    inner = lax.dot_general(
         left, right, (((1,), (1,)), ((), ())), preferred_element_type=F32
     )
-    dist = jnp.maximum(dist + right_norm, 0.0)
-    scaled = root_five * dist * lax.rsqrt(jnp.maximum(dist, 1e-30))
-    kern = (1.0 + scaled + (5.0 / 3.0) * dist) * jnp.exp(-scaled)
-    high = kern.astype(BF16)
-    return high, (kern - high.astype(F32)).astype(BF16)
+    for row in range(0, inner.shape[0], 16):
+        dist = jnp.maximum(inner[row : row + 16] + right_norm, 0.0)
+        scaled = root_five * dist * lax.rsqrt(jnp.maximum(dist, 1e-30))
+        kern = (1.0 + scaled + (5.0 / 3.0) * dist) * jnp.exp(-scaled)
+        high = kern.astype(BF16)
+        high_ref[at + row : at + row + 16, :] = high
+        low_ref[at + row : at + row + 16, :] = (kern - high.astype(F32)).astype(BF16)
 
 
 def pairs(slots):
@@ -130,7 +132,7 @@
 def kernel(
     rows, cols,
     train_hbm, cand_hbm, inv_hbm, noise_hbm, target_hbm,
-    solution_ref, mean_ref,
+    out_ref,
     train_ref, cand_ref, inv_ref, noise_ref, target_ref,
     lbuf, pbuf, cbuf, train_hi, train_lo, cand_hi, cand_lo,
     image_send, image_buf, vline, vplane, wsend, wbuf, first_ref, last_ref,
@@ -267,8 +269,7 @@
 
     def tile(slots, right, right_norm, high_ref, low_ref):
         left = jnp.concatenate([left_operand(lbuf[order[k], 0:32, :]) for k in slots], axis=0)
-        span = slice(64 * slots[0], 64 * slots[0] + 64 * len(slots))
-        high_ref[span, :], low_ref[span, :] = matern_split(left, right, right_norm)
+        matern_split(left, right, right_norm, high_ref, low_ref, 64 * slots[0])
 
     arrived(pbuf, p_recv)
     right_train, train_norm = right_operand([pbuf[s, 0:32, :] for s in range(plane)])
@@ -294,14 +295,6 @@
     first_ref[me] = spread([inner(partial, target_plane) + own_bnb, own_bb])
     to_all(first_ref, first_send, first_recv)
 
-    arrived(cbuf, c_recv)
-    right_cand, cand_norm = right_operand([cbuf[s] for s in range(plane)])
-    chunk = min(4, line // 2)
-    chunks = [list(range(at, at + chunk)) for at in range(0, line, chunk)]
-    half = len(chunks) // 2
-    for slots in chunks[:half]:
-        tile(slots, right_cand, cand_norm, cand_hi, cand_lo)
-
     arrived(image_buf, image_in)
     image = image_send[spot]
     for p in plane_peers:
@@ -314,8 +307,10 @@
     to_line(vline.at[z], vline, vl_send, vl_recv)
     to_plane(lambda p: vplane.at[spot], vplane, vp_send, vp_recv)
 
-    for slots in chunks[half:]:
-        tile(slots, right_cand, cand_norm, cand_hi, cand_lo)
+    arrived(cbuf, c_recv)
+    right_cand, cand_norm = right_operand([cbuf[s] for s in range(plane)])
+    for at in range(0, line, 4):
+        tile(list(range(at, min(line, at + 4))), right_cand, cand_norm, cand_hi, cand_lo)
     mean_b = applied(target_line, cand_hi, cand_lo)
 
     arrived(first_ref, first_recv)
@@ -330,6 +325,15 @@
     arrived(vline, vl_recv)
     residual_line = residuals(target_line, [vline[order[k]] for k in range(line)])
     image_r = applied(residual_line, train_hi, train_lo)
+    mean_r = applied(residual_line, cand_hi, cand_lo)
+    for s in range(plane):
+        at = 128 * (s // 2)
+        first, second = mean_b[:, at : at + 128], mean_r[:, at : at + 128]
+        if s % 2:
+            first = turned(first)
+        else:
+            second = turned(second)
+        wsend[s] = jnp.where(left16, first, second)
     arrived(vplane, vp_recv)
     residual_plane = residuals(target_plane, [vplane[s] for s in range(plane)])
     value_own = unpacked(value, value)[:, 0:64]
@@ -339,18 +343,8 @@
     own_rr = jnp.sum(square, axis=1, keepdims=True)
     own_vr = jnp.sum(value_own * residual_own, axis=1, keepdims=True)
     last_ref[me] = spread([own_rar, own_rr, own_vr])
+    to_plane(lambda p: wsend.at[p], wbuf, w_send, w_recv)
     to_all(last_ref, last_send, last_recv)
-
-    mean_r = applied(residual_line, cand_hi, cand_lo)
-    for s in range(plane):
-        at = 128 * (s // 2)
-        first, second = mean_b[:, at : at + 128], mean_r[:, at : at + 128]
-        if s % 2:
-            first = turned(first)
-        else:
-            second = turned(second)
-        wsend[s] = jnp.where(left16, first, second)
-    to_plane(lambda p: wsend.at[p], wbuf, w_send, w_recv)
 
     arrived(wbuf, w_recv)
     means = wsend[spot]
@@ -362,8 +356,8 @@
     curve = r_a_r + 2.0 * beta * v_r + beta * beta * b_a_b
     alpha_two = fresh / curve
     share = alpha + alpha_two * beta
-    solution_ref[...] = share * target + alpha_two * residual_own
-    mean_ref[...] = share * means[:, 0:64] + alpha_two * means[:, 64:128]
+    out_ref[0:16, :] = share * target + alpha_two * residual_own
+    out_ref[16:32, :] = share * means[:, 0:64] + alpha_two * means[:, 64:128]
     for copy in sent:
         copy.wait_send()
 
@@ -371,18 +365,18 @@
 def per_device(rows, cols, train_points, cand_points, inv_length, noise, targets):
     vmem = pl.BlockSpec(memory_space=pltpu.VMEM)
     hbm = pl.BlockSpec(memory_space=pltpu.HBM)
-    out = pltpu.VMEM(targets.shape, F32)
+    out = pltpu.VMEM((2 * targets.shape[0], targets.shape[1]), F32)
     operands = (
         train_points, cand_points, inv_length.reshape(1, -1), noise.reshape(1, -1), targets
     )
     dma = pltpu.SemaphoreType.DMA
     line, plane = rows // 2, 2 * cols
     kernel_tile = pltpu.VMEM((line * 64, plane * 64), BF16)
-    return pl.pallas_call(
+    both = pl.pallas_call(
         functools.partial(kernel, rows, cols),
-        out_shape=(out, out),
+        out_shape=out,
         in_specs=[hbm] * 5,
-        out_specs=(vmem, vmem),
+        out_specs=vmem,
         scratch_shapes=[pltpu.VMEM(operand.shape, F32) for operand in operands]
         + [
             pltpu.VMEM((line, 48, 128), BF16),
@@ -404,6 +398,7 @@
             collective_id=0, has_side_effects=True, vmem_limit_bytes=60 * 1024 * 1024
         ),
     )(*operands)
+    return both[:16], both[16:]
 
 
 def solution(mesh):

time: 25 us -> 24.6 us (0.984)
  local copies, waits for them, and re-layouts: 1.2 us -> 0.61 us
    unnamed x2 -> x0, local copies, waits for them, and re-layouts: 1.2 us -> none
    slice x0 -> x1, local copies, waits for them, and re-layouts: none -> 0.61 us  [per_device(): return (both[:16], both[16:])]
where the time goes in v5:
time: 24.6 us; the launch traced here: 24.4 us
  Pallas kernels  23.1 us (94%)
  between operations  0.64 us (3%)
  local copies, waits for them, and re-layouts  0.61 us (2%)
    pallas_call x1, Pallas kernels, per_device(): pl.pallas_call(functools.partial(kernel, rows, cols), out_shape=out, in_s...  23.1 us
    slice x1, local copies, waits for them, and re-layouts, per_device(): return (both[:16], both[16:])  0.61 us

profile of v5, /device:TPU:0, one launch (start us, length us, event | category | flops | bytes accessed | tf_op | source)
XLA Modules:
  0.0 24.4 jit_solution(7593084712386399703)
XLA Ops:
  0.6 23.1 %shard_map.68 = f32[32,64]{1,0:T(8,128)S(1)} custom-call(f32[64,64]{1,0:T(8,128)} %train_hbm.1, f32[64,64]{1,0:T(8,128)} %cand_hbm.1, f32[1,64]{1,0:T(1,128)} %bitcast.2, f32[1,64]{1,0:T(1,128)} %bitcast.3, f32[16,64]{1,0:T(8,128)} %target_hbm.1), custom_call_target="tpu_custom_call" | custom-call | tf_op jit(solution)/shard_map/pallas_call | solution.py:375
  23.8 0.6 %fusion = (f32[16,64]{1,0:T(8,128)}, f32[16,64]{1,0:T(8,128)}) fusion(f32[32,64]{1,0:T(8,128)S(1)} %shard_map.68), kind=kLoop, calls=%fused_computation | loop fusion | bytes 16384 | tf_op jit(solution)/shard_map/slice | solution.py:401

commit v6 on v5

--- a/solution.py
+++ b/solution.py
@@ -8,7 +8,7 @@
 from jax.experimental.pallas import tpu as pltpu
 from jax.sharding import PartitionSpec as P
 
-MESH = pl.DeviceIdType.MESH
+LOGICAL = pl.DeviceIdType.LOGICAL
 root_five = math.sqrt(5.0)
 F32 = jnp.float32
 BF16 = jnp.bfloat16
@@ -158,22 +158,23 @@
     a = lax.axis_index("row")
     b = lax.axis_index("col")
     devices = rows * cols
-    me = a * cols + b
-    z, core = lax.div(a, 2), lax.rem(a, 2)
     line, plane = rows // 2, 2 * cols
-    spot = core * cols + b
+    z = lax.div(a, 2)
+    spot = lax.rem(a, 2) * cols + b
+    me = z * plane + spot
     line_peers = [lax.rem(z + k, line) for k in range(1, line)]
     plane_peers = [lax.rem(spot + k, plane) for k in range(1, plane)]
     order = [z] + [lax.rem(z + line - k, line) for k in range(1, line)]
 
+    apart = sorted(range(1, devices), key=lambda k: abs(k - devices // 2))
+
     def each_other(act):
         def step(k, carry):
-            other = lax.rem(me + k, devices)
-            act((lax.div(other, cols), lax.rem(other, cols)))
+            act(lax.rem(me + k, devices))
             return carry
 
         if devices <= 64:
-            for k in range(1, devices):
+            for k in apart:
                 step(k, 0)
         else:
             lax.fori_loop(1, devices, step, 0)
@@ -181,7 +182,7 @@
     barrier = pltpu.get_barrier_semaphore()
     each_other(
         lambda device: pl.semaphore_signal(
-            barrier, inc=1, device_id=device, device_id_type=MESH
+            barrier, inc=1, device_id=device, device_id_type=LOGICAL
         )
     )
 
@@ -190,25 +191,24 @@
     def start(src, dst, send, recv, device):
         pltpu.make_async_remote_copy(
             src_ref=src, dst_ref=dst, send_sem=send, recv_sem=recv,
-            device_id=device, device_id_type=MESH,
+            device_id=device, device_id_type=LOGICAL,
         ).start()
 
     def blocks(buf, amount, sem):
         span = buf.at[pl.ds(0, amount)]
         return pltpu.make_async_remote_copy(
             src_ref=span, dst_ref=span, send_sem=sem, recv_sem=sem,
-            device_id=(a, b), device_id_type=MESH,
+            device_id=me, device_id_type=LOGICAL,
         )
 
     def to_line(src, buf, send, recv):
         for p in line_peers:
-            start(src, buf.at[z], send, recv, (2 * p + core, b))
+            start(src, buf.at[z], send, recv, p * plane + spot)
         sent.append(blocks(buf, line - 1, send))
 
     def to_plane(src, buf, send, recv):
         for p in plane_peers:
-            device = (2 * z + lax.div(p, cols), lax.rem(p, cols))
-            start(src(p), buf.at[spot], send, recv, device)
+            start(src(p), buf.at[spot], send, recv, z * plane + p)
         sent.append(blocks(buf, plane - 1, send))
 
     def to_all(buf, send, recv):
@@ -257,7 +257,7 @@
     pbuf[spot, 32:48, :] = target_block
     pl.semaphore_wait(barrier, devices - 1)
     for p in line_peers:
-        start(lbuf.at[z], lbuf.at[z], l_send, l_recv.at[z], (2 * p + core, b))
+        start(lbuf.at[z], lbuf.at[z], l_send, l_recv.at[z], p * plane + spot)
     sent.append(blocks(lbuf, line - 1, l_send))
     to_plane(lambda p: pbuf.at[spot], pbuf, p_send, p_recv)
     loads[3].wait()
@@ -280,7 +280,7 @@
             p = order[k]
             pltpu.make_async_remote_copy(
                 src_ref=lbuf.at[p], dst_ref=lbuf.at[p], send_sem=l_send, recv_sem=l_recv.at[p],
-                device_id=(a, b), device_id_type=MESH,
+                device_id=me, device_id_type=LOGICAL,
             ).wait_recv()
         tile(slots, right_train, train_norm, train_hi, train_lo)
     target_line = pairs([whole(lbuf[order[k], 32:48, :]) for k in range(line)])
@@ -343,8 +343,8 @@
     own_rr = jnp.sum(square, axis=1, keepdims=True)
     own_vr = jnp.sum(value_own * residual_own, axis=1, keepdims=True)
     last_ref[me] = spread([own_rar, own_rr, own_vr])
+    to_all(last_ref, last_send, last_recv)
     to_plane(lambda p: wsend.at[p], wbuf, w_send, w_recv)
-    to_all(last_ref, last_send, last_recv)
 
     arrived(wbuf, w_recv)
     means = wsend[spot]

time: 24.6 us -> 24.6 us (level)
  no operation moved by 1% of the time
where the time goes in v6:
time: 24.6 us; the launch traced here: 24.5 us
  Pallas kernels  23.2 us (94%)
  between operations  0.64 us (3%)
  local copies, waits for them, and re-layouts  0.61 us (2%)
    pallas_call x1, Pallas kernels, per_device(): pl.pallas_call(functools.partial(kernel, rows, cols), out_shape=out, in_s...  23.2 us
    slice x1, local copies, waits for them, and re-layouts, per_device(): return (both[:16], both[16:])  0.61 us

profile of v6, /device:TPU:0, one launch (start us, length us, event | category | flops | bytes accessed | tf_op | source)
XLA Modules:
  0.0 24.5 jit_solution(16983490373035705838)
XLA Ops:
  0.6 23.2 %shard_map.68 = f32[32,64]{1,0:T(8,128)S(1)} custom-call(f32[64,64]{1,0:T(8,128)} %train_hbm.1, f32[64,64]{1,0:T(8,128)} %cand_hbm.1, f32[1,64]{1,0:T(1,128)} %bitcast.2, f32[1,64]{1,0:T(1,128)} %bitcast.3, f32[16,64]{1,0:T(8,128)} %target_hbm.1), custom_call_target="tpu_custom_call" | custom-call | tf_op jit(solution)/shard_map/pallas_call | solution.py:375
  23.9 0.6 %fusion = (f32[16,64]{1,0:T(8,128)}, f32[16,64]{1,0:T(8,128)}) fusion(f32[32,64]{1,0:T(8,128)S(1)} %shard_map.68), kind=kLoop, calls=%fused_computation | loop fusion | bytes 16384 | tf_op jit(solution)/shard_map/slice | solution.py:401

commit v7 on v6

--- a/solution.py
+++ b/solution.py
@@ -94,17 +94,23 @@
     return operand, summed[0:1]
 
 
-def matern_split(left, right, right_norm, high_ref, low_ref, at):
-    inner = lax.dot_general(
+def matern_split(left, right, right_norm, inner_ref, high_ref, low_ref, at):
+    amount = left.shape[0]
+    inner_ref[0:amount, :] = lax.dot_general(
         left, right, (((1,), (1,)), ((), ())), preferred_element_type=F32
     )
-    for row in range(0, inner.shape[0], 16):
-        dist = jnp.maximum(inner[row : row + 16] + right_norm, 0.0)
+
+    def strip(index, carry):
+        row = pl.multiple_of(index * 32, 32)
+        dist = jnp.maximum(inner_ref[pl.ds(row, 32), :] + right_norm, 0.0)
         scaled = root_five * dist * lax.rsqrt(jnp.maximum(dist, 1e-30))
         kern = (1.0 + scaled + (5.0 / 3.0) * dist) * jnp.exp(-scaled)
         high = kern.astype(BF16)
-        high_ref[at + row : at + row + 16, :] = high
-        low_ref[at + row : at + row + 16, :] = (kern - high.astype(F32)).astype(BF16)
+        high_ref[pl.ds(at + row, 32), :] = high
+        low_ref[pl.ds(at + row, 32), :] = (kern - high.astype(F32)).astype(BF16)
+        return carry
+
+    lax.fori_loop(0, amount // 32, strip, 0)
 
 
 def pairs(slots):
@@ -134,7 +140,7 @@
     train_hbm, cand_hbm, inv_hbm, noise_hbm, target_hbm,
     out_ref,
     train_ref, cand_ref, inv_ref, noise_ref, target_ref,
-    lbuf, pbuf, cbuf, train_hi, train_lo, cand_hi, cand_lo,
+    lbuf, pbuf, cbuf, inner_ref, train_hi, train_lo, cand_hi, cand_lo,
     image_send, image_buf, vline, vplane, wsend, wbuf, first_ref, last_ref,
     in_sem, l_recv,
     l_send, p_send, p_recv, c_send, c_recv, image_out, image_in,
@@ -166,18 +172,15 @@
     plane_peers = [lax.rem(spot + k, plane) for k in range(1, plane)]
     order = [z] + [lax.rem(z + line - k, line) for k in range(1, line)]
 
-    apart = sorted(range(1, devices), key=lambda k: abs(k - devices // 2))
+    def each_peer(mine, amount, act):
+        def step(k, carry):
+            act(lax.rem(mine + k, amount))
+            return carry
+
+        lax.fori_loop(1, amount, step, 0)
 
     def each_other(act):
-        def step(k, carry):
-            act(lax.rem(me + k, devices))
-            return carry
-
-        if devices <= 64:
-            for k in apart:
-                step(k, 0)
-        else:
-            lax.fori_loop(1, devices, step, 0)
+        each_peer(me, devices, act)
 
     barrier = pltpu.get_barrier_semaphore()
     each_other(
@@ -202,13 +205,13 @@
         )
 
     def to_line(src, buf, send, recv):
-        for p in line_peers:
-            start(src, buf.at[z], send, recv, p * plane + spot)
+        each_peer(z, line, lambda p: start(src, buf.at[z], send, recv, p * plane + spot))
         sent.append(blocks(buf, line - 1, send))
 
     def to_plane(src, buf, send, recv):
-        for p in plane_peers:
-            start(src(p), buf.at[spot], send, recv, z * plane + p)
+        each_peer(
+            spot, plane, lambda p: start(src(p), buf.at[spot], send, recv, z * plane + p)
+        )
         sent.append(blocks(buf, plane - 1, send))
 
     def to_all(buf, send, recv):
@@ -256,9 +259,7 @@
     pbuf[spot, 0:32, :] = own_train
     pbuf[spot, 32:48, :] = target_block
     pl.semaphore_wait(barrier, devices - 1)
-    for p in line_peers:
-        start(lbuf.at[z], lbuf.at[z], l_send, l_recv.at[z], p * plane + spot)
-    sent.append(blocks(lbuf, line - 1, l_send))
+    to_line(lbuf.at[z], lbuf, l_send, l_recv.at[z])
     to_plane(lambda p: pbuf.at[spot], pbuf, p_send, p_recv)
     loads[3].wait()
     cbuf[spot] = points_of(cand_ref)
@@ -269,7 +270,7 @@
 
     def tile(slots, right, right_norm, high_ref, low_ref):
         left = jnp.concatenate([left_operand(lbuf[order[k], 0:32, :]) for k in slots], axis=0)
-        matern_split(left, right, right_norm, high_ref, low_ref, 64 * slots[0])
+        matern_split(left, right, right_norm, inner_ref, high_ref, low_ref, 64 * slots[0])
 
     arrived(pbuf, p_recv)
     right_train, train_norm = right_operand([pbuf[s, 0:32, :] for s in range(plane)])
@@ -382,6 +383,7 @@
             pltpu.VMEM((line, 48, 128), BF16),
             pltpu.VMEM((plane, 48, 128), BF16),
             pltpu.VMEM((plane, 32, 128), BF16),
+            pltpu.VMEM((64 * min(4, line), plane * 64), F32),
             kernel_tile, kernel_tile, kernel_tile, kernel_tile,
             pltpu.VMEM((plane, 8, 128), F32),
             pltpu.VMEM((plane, 8, 128), F32),

time: 24.6 us -> 24.8 us (level)
  no operation moved by 1% of the time
where the time goes in v7:
time: 24.8 us; the launch traced here: 24.6 us
  Pallas kernels  23.4 us (94%)
  between operations  0.64 us (3%)
  local copies, waits for them, and re-layouts  0.61 us (2%)
    pallas_call x1, Pallas kernels, per_device(): pl.pallas_call(functools.partial(kernel, rows, cols), out_shape=out, in_s...  23.4 us
    slice x1, local copies, waits for them, and re-layouts, per_device(): return (both[:16], both[16:])  0.61 us

profile of v7, /device:TPU:0, one launch (start us, length us, event | category | flops | bytes accessed | tf_op | source)
XLA Modules:
  0.0 24.6 jit_solution(6589356204106512014)
XLA Ops:
  0.6 23.4 %shard_map.68 = f32[32,64]{1,0:T(8,128)S(1)} custom-call(f32[64,64]{1,0:T(8,128)} %train_hbm.1, f32[64,64]{1,0:T(8,128)} %cand_hbm.1, f32[1,64]{1,0:T(1,128)} %bitcast.2, f32[1,64]{1,0:T(1,128)} %bitcast.3, f32[16,64]{1,0:T(8,128)} %target_hbm.1), custom_call_target="tpu_custom_call" | custom-call | tf_op jit(solution)/shard_map/pallas_call | solution.py:376
  24.0 0.6 %fusion = (f32[16,64]{1,0:T(8,128)}, f32[16,64]{1,0:T(8,128)}) fusion(f32[32,64]{1,0:T(8,128)S(1)} %shard_map.68), kind=kLoop, calls=%fused_computation | loop fusion | bytes 16384 | tf_op jit(solution)/shard_map/slice | solution.py:403

commit v8 on v6

--- a/solution.py
+++ b/solution.py
@@ -135,11 +135,11 @@
     out_ref,
     train_ref, cand_ref, inv_ref, noise_ref, target_ref,
     lbuf, pbuf, cbuf, train_hi, train_lo, cand_hi, cand_lo,
-    image_send, image_buf, vline, vplane, wsend, wbuf, first_ref, last_ref,
+    image_send, image_buf, vline, vplane, wsend, wbuf, last_ref,
     in_sem, l_recv,
     l_send, p_send, p_recv, c_send, c_recv, image_out, image_in,
     vl_send, vl_recv, vp_send, vp_recv, w_send, w_recv,
-    first_send, first_recv, last_send, last_recv,
+    last_send, last_recv,
 ):
     loads = [
         pltpu.make_async_copy(src, dst, in_sem.at[n])
@@ -232,8 +232,8 @@
             total = jnp.where(lane == row_at + 16 * q, one, total)
         return jnp.sum(total, axis=0, keepdims=True)
 
-    def gathered(ref, amount):
-        total = jnp.sum(ref[...], axis=0)
+    def gathered(rows_in, amount):
+        total = jnp.sum(rows_in, axis=0)
         return [
             jnp.sum(jnp.where(lane == row_at + 16 * q, total, 0.0), axis=1, keepdims=True)
             for q in range(amount)
@@ -285,15 +285,15 @@
         tile(slots, right_train, train_norm, train_hi, train_lo)
     target_line = pairs([whole(lbuf[order[k], 32:48, :]) for k in range(line)])
     partial = applied(target_line, train_hi, train_lo)
-    for s in range(plane):
-        image_send[s] = packed(partial[:, 128 * (s // 2) : 128 * (s // 2) + 128], s % 2)
-    to_plane(lambda p: image_send.at[p], image_buf, image_out, image_in)
-
     target_plane = pairs([whole(pbuf[s, 32:48, :]) for s in range(plane)])
     own_bb = jnp.sum(target * target, axis=1, keepdims=True)
     own_bnb = jnp.sum(noise * target * target, axis=1, keepdims=True)
-    first_ref[me] = spread([inner(partial, target_plane) + own_bnb, own_bb])
-    to_all(first_ref, first_send, first_recv)
+    first = spread([inner(partial, target_plane) + own_bnb, own_bb])
+    first = jnp.broadcast_to(first, (8, 128))
+    for s in range(plane):
+        image_send[s, 0:8, :] = packed(partial[:, 128 * (s // 2) : 128 * (s // 2) + 128], s % 2)
+        image_send[s, 8:16, :] = first
+    to_plane(lambda p: image_send.at[p], image_buf, image_out, image_in)
 
     arrived(image_buf, image_in)
     image = image_send[spot]
@@ -301,8 +301,9 @@
         image += image_buf[p]
     left8 = in_left(8)
     target_packed = jnp.where(left8, target2[0:8], target2[8:16])
-    value = image + noise2 * target_packed
-    vline[z] = value
+    value = image[0:8] + noise2 * target_packed
+    vline[z, 0:8, :] = value
+    vline[z, 8:16, :] = image[8:16]
     vplane[spot] = value
     to_line(vline.at[z], vline, vl_send, vl_recv)
     to_plane(lambda p: vplane.at[spot], vplane, vp_send, vp_recv)
@@ -313,8 +314,8 @@
         tile(list(range(at, min(line, at + 4))), right_cand, cand_norm, cand_hi, cand_lo)
     mean_b = applied(target_line, cand_hi, cand_lo)
 
-    arrived(first_ref, first_recv)
-    b_a_b, b_b = gathered(first_ref, 2)
+    arrived(vline, vl_recv)
+    b_a_b, b_b = gathered(vline[:, 8:16, :][:, 0:1, :], 2)
     alpha = b_b / b_a_b
 
     def residuals(target_blocks, slots):
@@ -322,8 +323,7 @@
             block - alpha * values for block, values in zip(target_blocks, unpacked_pairs(slots))
         ]
 
-    arrived(vline, vl_recv)
-    residual_line = residuals(target_line, [vline[order[k]] for k in range(line)])
+    residual_line = residuals(target_line, [vline[order[k], 0:8, :] for k in range(line)])
     image_r = applied(residual_line, train_hi, train_lo)
     mean_r = applied(residual_line, cand_hi, cand_lo)
     for s in range(plane):
@@ -351,7 +351,7 @@
     for p in plane_peers:
         means += wbuf[p]
     arrived(last_ref, last_recv)
-    r_a_r, fresh, v_r = gathered(last_ref, 3)
+    r_a_r, fresh, v_r = gathered(last_ref[...], 3)
     beta = fresh / b_b
     curve = r_a_r + 2.0 * beta * v_r + beta * beta * b_a_b
     alpha_two = fresh / curve
@@ -383,17 +383,16 @@
             pltpu.VMEM((plane, 48, 128), BF16),
             pltpu.VMEM((plane, 32, 128), BF16),
             kernel_tile, kernel_tile, kernel_tile, kernel_tile,
-            pltpu.VMEM((plane, 8, 128), F32),
-            pltpu.VMEM((plane, 8, 128), F32),
-            pltpu.VMEM((line, 8, 128), F32),
+            pltpu.VMEM((plane, 16, 128), F32),
+            pltpu.VMEM((plane, 16, 128), F32),
+            pltpu.VMEM((line, 16, 128), F32),
             pltpu.VMEM((plane, 8, 128), F32),
             pltpu.VMEM((plane, 16, 128), F32),
             pltpu.VMEM((plane, 16, 128), F32),
             pltpu.VMEM((rows * cols, 1, 128), F32),
-            pltpu.VMEM((rows * cols, 1, 128), F32),
             dma((5,)), dma((line,)),
         ]
-        + [dma] * 17,
+        + [dma] * 15,
         compiler_params=pltpu.CompilerParams(
             collective_id=0, has_side_effects=True, vmem_limit_bytes=60 * 1024 * 1024
         ),

time: 24.6 us -> 25 us (1.016)
  Pallas kernels: 23.2 us -> 23.5 us
    pallas_call x1, Pallas kernels: 23.2 us -> 23.5 us  [per_device(): pl.pallas_call(functools.partial(kernel, rows, cols), out_shape=out, in_s...]
where the time goes in v8:
time: 25 us; the launch traced here: 24.8 us
  Pallas kernels  23.5 us (94%)
  between operations  0.64 us (3%)
  local copies, waits for them, and re-layouts  0.61 us (2%)
    pallas_call x1, Pallas kernels, per_device(): pl.pallas_call(functools.partial(kernel, rows, cols), out_shape=out, in_s...  23.5 us
    slice x1, local copies, waits for them, and re-layouts, per_device(): return (both[:16], both[16:])  0.61 us

profile of v8, /device:TPU:0, one launch (start us, length us, event | category | flops | bytes accessed | tf_op | source)
XLA Modules:
  0.0 24.8 jit_solution(6877484554980199382)
XLA Ops:
  0.6 23.5 %shard_map.68 = f32[32,64]{1,0:T(8,128)S(1)} custom-call(f32[64,64]{1,0:T(8,128)} %train_hbm.1, f32[64,64]{1,0:T(8,128)} %cand_hbm.1, f32[1,64]{1,0:T(1,128)} %bitcast.2, f32[1,64]{1,0:T(1,128)} %bitcast.3, f32[16,64]{1,0:T(8,128)} %target_hbm.1), custom_call_target="tpu_custom_call" | custom-call | tf_op jit(solution)/shard_map/pallas_call | solution.py:375
  24.2 0.6 %fusion = (f32[16,64]{1,0:T(8,128)}, f32[16,64]{1,0:T(8,128)}) fusion(f32[32,64]{1,0:T(8,128)S(1)} %shard_map.68), kind=kLoop, calls=%fused_computation | loop fusion | bytes 16384 | tf_op jit(solution)/shard_map/slice | solution.py:400

commit v9 on v5

--- a/solution.py
+++ b/solution.py
@@ -292,8 +292,11 @@
     target_plane = pairs([whole(pbuf[s, 32:48, :]) for s in range(plane)])
     own_bb = jnp.sum(target * target, axis=1, keepdims=True)
     own_bnb = jnp.sum(noise * target * target, axis=1, keepdims=True)
-    first_ref[me] = spread([inner(partial, target_plane) + own_bnb, own_bb])
-    to_all(first_ref, first_send, first_recv)
+
+    arrived(cbuf, c_recv)
+    right_cand, cand_norm = right_operand([cbuf[s] for s in range(plane)])
+    for at in range(0, line, 4):
+        tile(list(range(at, min(line, at + 4))), right_cand, cand_norm, cand_hi, cand_lo)
 
     arrived(image_buf, image_in)
     image = image_send[spot]
@@ -307,10 +310,8 @@
     to_line(vline.at[z], vline, vl_send, vl_recv)
     to_plane(lambda p: vplane.at[spot], vplane, vp_send, vp_recv)
 
-    arrived(cbuf, c_recv)
-    right_cand, cand_norm = right_operand([cbuf[s] for s in range(plane)])
-    for at in range(0, line, 4):
-        tile(list(range(at, min(line, at + 4))), right_cand, cand_norm, cand_hi, cand_lo)
+    first_ref[me] = spread([inner(partial, target_plane) + own_bnb, own_bb])
+    to_all(first_ref, first_send, first_recv)
     mean_b = applied(target_line, cand_hi, cand_lo)
 
     arrived(first_ref, first_recv)

time: 24.6 us -> 26.2 us (1.065)
  Pallas kernels: 23.1 us -> 24.8 us
    pallas_call x1, Pallas kernels: 23.1 us -> 24.8 us  [per_device(): pl.pallas_call(functools.partial(kernel, rows, cols), out_shape=out, in_s...]
where the time goes in v9:
time: 26.2 us; the launch traced here: 26 us
  Pallas kernels  24.8 us (95%)
  between operations  0.64 us (2%)
  local copies, waits for them, and re-layouts  0.61 us (2%)
    pallas_call x1, Pallas kernels, per_device(): pl.pallas_call(functools.partial(kernel, rows, cols), out_shape=out, in_s...  24.8 us
    slice x1, local copies, waits for them, and re-layouts, per_device(): return (both[:16], both[16:])  0.61 us

profile of v9, /device:TPU:0, one launch (start us, length us, event | category | flops | bytes accessed | tf_op | source)
XLA Modules:
  0.0 26.0 jit_solution(9213426047675425628)
XLA Ops:
  0.6 24.8 %shard_map.68 = f32[32,64]{1,0:T(8,128)S(1)} custom-call(f32[64,64]{1,0:T(8,128)} %train_hbm.1, f32[64,64]{1,0:T(8,128)} %cand_hbm.1, f32[1,64]{1,0:T(1,128)} %bitcast.2, f32[1,64]{1,0:T(1,128)} %bitcast.3, f32[16,64]{1,0:T(8,128)} %target_hbm.1), custom_call_target="tpu_custom_call" | custom-call | tf_op jit(solution)/shard_map/pallas_call | solution.py:376
  25.4 0.6 %fusion = (f32[16,64]{1,0:T(8,128)}, f32[16,64]{1,0:T(8,128)}) fusion(f32[32,64]{1,0:T(8,128)S(1)} %shard_map.68), kind=kLoop, calls=%fused_computation | loop fusion | bytes 16384 | tf_op jit(solution)/shard_map/slice | solution.py:402
